TPU v7x, 768 devices: a whole 4x8x12 slice. The times are simulated.
768 devices in a mesh: section: 24 (over y_hi, z), fsdp: 8 (over y_lo, core), tensor: 4 (over x).
Axes of the slice: x: 4, y: 8 (y_hi: 2, y_lo: 4; y = y_hi * 4 + y_lo), z: 12, core: 2. Of those that a mesh axis runs over, the one named last changes fastest.
Arguments:
- fresh: bfloat16 [2, 512, 2560], P(None, 'fsdp'), may hold values from -6 to 6
- sent: bfloat16 [24, 512, 2560], P('section', 'fsdp'), may hold values from -6 to 6
- stash: bfloat16 [24, 2, 512, 2560], P('section', None, 'fsdp'), may hold values from -6 to 6
- returned: bfloat16 [24, 512, 2560], P('section', 'fsdp'), may hold values from -6 to 6
- loss_grads: bfloat16 [2, 512, 2560], P(None, 'fsdp'), may hold values from -6 to 6
- plan: int32 [24, 2], P('section'), may hold values from 0 to 1
- frame_ids: int32 [2, 512], P(None, 'fsdp'), may hold values from 0 to 63, never falling along the last dimension, each value on 1 to 16 neighbouring positions
- qkv_weight: bfloat16 [24, 2560, 4096], P('section', 'fsdp', 'tensor'), may hold values from -0.125 to 0.125
- out_weight: bfloat16 [24, 2560, 2048], P('section', 'fsdp', 'tensor'), may hold values from -0.125 to 0.125
Outputs:
- activations_out: bfloat16 [24, 512, 2560], P('section', 'fsdp')
- cotangents_out: bfloat16 [24, 512, 2560], P('section', 'fsdp')
Inputs may be any that keep to these rules, and one draw needn't show every extreme that they name: `frame_ids`: frame numbers never fall along the tokens; a frame holds 1 to 16 tokens, and some frame holds exactly 16.
All inputs are finite; a program needn't handle non-finite values.
Results may differ from a plain program's by a relative error of at most 0.02.
Values may be sent and summed in bfloat16 or wider, within the bound.
A program may use at most 64 MiB of HBM per device.

v0:
```python
import jax
import jax.numpy as jnp
from jax import lax
from jax.sharding import PartitionSpec as P

HS = 128


def passed_along(value, axis, steps):
    count = lax.axis_size(axis)
    initial, last = (max(0, -steps), min(count, count - steps))
    return lax.ppermute(value, axis, [(source, source + steps) for source in range(initial, last)])


def group_partial(x, wq, wo, frames):
    q_heads = wo.shape[1] // HS
    kv_heads = (wq.shape[1] // HS - q_heads) // 2
    rows = x.shape[0]
    xf = x.astype(jnp.float32)
    normed = (xf * lax.rsqrt(jnp.mean(xf * xf, -1, keepdims=True) + 1e-05)).astype(jnp.bfloat16)
    mixed = jnp.dot(normed, wq, preferred_element_type=jnp.float32).astype(jnp.bfloat16)
    mixed = mixed.reshape(rows, q_heads + 2 * kv_heads, HS)
    query = mixed[:, :q_heads].reshape(rows, kv_heads, q_heads // kv_heads, HS)
    keys = mixed[:, q_heads : q_heads + kv_heads]
    values = mixed[:, q_heads + kv_heads :]
    scores = jnp.einsum("tkgd,skd->kgts", query, keys, preferred_element_type=jnp.float32) * HS ** (
        -0.5
    )
    allowed = frames[None, :] <= frames[:, None]
    weights = jnp.where(allowed, jnp.exp(scores), 0.0)
    probs = (weights / jnp.sum(weights, -1, keepdims=True)).astype(jnp.bfloat16)
    context = jnp.einsum("kgts,skd->tkgd", probs, values, preferred_element_type=jnp.float32)
    context = context.astype(jnp.bfloat16).reshape(rows, q_heads * HS)
    return lax.dot_general(
        context, wo, (((1,), (1,)), ((), ())), preferred_element_type=jnp.float32
    )


def back_partial(x, grad, wq, wo, frames):
    _, pull = jax.vjp(lambda a: group_partial(a, wq, wo, frames), x)
    return pull(grad.astype(jnp.float32))[0].astype(jnp.float32)


def body(fresh, sent, stash, returned, loss_grads, plan, frame_ids, qkv_weight, out_weight):
    section = lax.axis_index("section")
    count = lax.axis_size("section")
    first = section == 0
    final = section == count - 1
    wq_full, wo_full = (
        lax.all_gather(qkv_weight, "fsdp", axis=1, tiled=True),
        lax.all_gather(out_weight, "fsdp", axis=1, tiled=True),
    )
    wq_local = wq_full[0]
    wo_local = wo_full[0]

    def move_down(acts):
        return passed_along(acts, "section", 1)

    def move_up(cots):
        return passed_along(cots, "section", -1)

    def layer_forward(x, frames):
        total = lax.psum(
            group_partial(x, wq_local, wo_local, frames).astype(jnp.bfloat16), "tensor"
        ).astype(jnp.float32)
        return (x.astype(jnp.float32) + total).astype(jnp.bfloat16)

    def layer_backward(x, grad, frames):
        total = lax.psum(
            back_partial(x, grad, wq_local, wo_local, frames).astype(jnp.bfloat16), "tensor"
        ).astype(jnp.float32)
        return (grad.astype(jnp.float32) + total).astype(jnp.bfloat16)

    start_down = sent[0]
    start_up = returned[0]

    def forward_tick(tick, incoming):
        inputs = jnp.where(first, fresh[tick], incoming)
        return layer_forward(inputs, frame_ids[tick])

    def backward_tick(tick, incoming):
        grad = jnp.where(final, loss_grads[tick], incoming)
        slot = plan[0, tick]
        saved = lax.dynamic_index_in_dim(stash[0], slot, 0, keepdims=False)
        marks = lax.dynamic_index_in_dim(frame_ids, slot, 0, keepdims=False)
        return layer_backward(saved, grad, marks)

    first_out = forward_tick(0, move_down(start_down))
    first_back = backward_tick(0, move_up(start_up))
    second_out = forward_tick(1, move_down(first_out))
    second_back = backward_tick(1, move_up(first_back))
    return (second_out[None], second_back[None])


def solution(mesh):
    placed = (
        P(None, "fsdp", None),
        P("section", "fsdp", None),
        P("section", None, "fsdp", None),
        P("section", "fsdp", None),
        P(None, "fsdp", None),
        P("section", None),
        P(None, "fsdp"),
        P("section", "fsdp", "tensor"),
        P("section", "fsdp", "tensor"),
    )
    return jax.shard_map(
        body,
        mesh=mesh,
        in_specs=placed,
        out_specs=(P("section", "fsdp", None), P("section", "fsdp", None)),
        check_vma=False,
    )
```

profile of v0, /device:TPU:56, one launch (start us, length us, event | category | flops | bytes accessed | tf_op | source)
XLA Modules:
  0.0 317.3 jit_solution(7073603838384121449)
XLA Ops:
  7.2 0.7 all-gather.5.cloned.1.call-update
  8.0 0.7 all-gather.3.cloned.1.call-update
  8.7 4.3 %collective-permute-start = (bf16[64,2560]{1,0:T(8,128)(2,1)}, bf16[64,2560]{1,0:T(8,128)(2,1)S(1)}, u32[]{:S(2)}, u32[]{:S(2)}) collective-permute-start(bf16[64,2560]{1,0:T(8,128)(2,1)} %bitcast.364), channel_id=1, source_target_pairs={{0,32},{32,64},{64,96},{96,128},{128,160},{160,192},{192,224},{224... | collective-permute-start | bytes 983048 | tf_op jit(solution)/shard_map/ppermute | solution.py:12
  13.0 14.5 %collective-permute-start.2 = (bf16[64,2560]{1,0:T(8,128)(2,1)}, bf16[64,2560]{1,0:T(8,128)(2,1)S(1)}, u32[]{:S(2)}, u32[]{:S(2)}) collective-permute-start(bf16[64,2560]{1,0:T(8,128)(2,1)} %bitcast.365), channel_id=1, source_target_pairs={{32,0},{64,32},{96,64},{128,96},{160,128},{192,160},{224,192},{256... | collective-permute-start | bytes 983048 | tf_op jit(solution)/shard_map/ppermute | solution.py:12
  27.5 1.3 fusion.166
  32.7 1.2 fusion.86
  33.8 0.8 fusion.147
  34.7 0.7 broadcast_compare_fusion
  35.7 2.9 collective-permute-done
  38.6 1.2 fusion.92
  39.8 22.1 %all-gather.5.cloned.1.call-done = bf16[1,2560,512]{2,1,0:T(8,128)(2,1)} async-done(((bf16[1,320,512]{2,1,0:T(8,128)(2,1)}), bf16[1,2560,512]{2,1,0:T(8,128)(2,1)}) %all-gather.5.cloned.1.call-update) | async-done | bytes 2621456 | tf_op jit(solution)/shard_map/all_gather | solution.py:51
  61.9 2.4 fusion.62
  64.4 66.6 %all-gather.3.cloned.1.call-done = bf16[1,2560,1024]{2,1,0:T(8,128)(2,1)} async-done(((bf16[1,320,1024]{2,1,0:T(8,128)(2,1)}), bf16[1,2560,1024]{2,1,0:T(8,128)(2,1)}) %all-gather.3.cloned.1.call-update) | async-done | bytes 5242896 | tf_op jit(solution)/shard_map/all_gather | solution.py:50
  131.0 3.7 %fusion.45 = bf16[8,8,8,128]{3,1,2,0:T(8,128)(2,1)S(1)} fusion(bf16[1,2560,1024]{2,1,0:T(8,128)(2,1)} %all-gather.3.cloned.1.call-done, f32[64]{0:T(128)S(1)} %fusion.148, bf16[1,2,64,2560]{3,2,1,0:T(8,128)(2,1)S(1)} %copy-done.2, s32[]{:T(128)S(6)} %select_n.62), kind=kOutput, calls=%fused_computation.29 | convolution fusion | flops 336101376 | bytes 5702148 | tf_op jit(solution)/shard_map/jvp()/dot_general | solution.py:21
  135.0 1.1 fusion.51
  136.2 0.2 fusion.126
  136.7 0.2 multiply_reduce_fusion.1
  136.9 0.2 fusion.79
  137.1 0.2 convolution_convert_fusion.7
  137.6 0.2 fusion.70
  137.9 4.4 %fusion.87 = (f32[64]{0:T(128)S(1)}, f32[64]{0:T(128)S(1)}, f32[64,2560]{1,0:T(8,128)S(1)}) fusion(bf16[1,2,64,2560]{3,2,1,0:T(8,128)(2,1)S(1)} %copy-done.2, s32[]{:T(128)S(6)} %select_n.62, s32[]{:T(128)S(6)} %select_n.66, bf16[1,2560,1024]{2,1,0:T(8,128)(2,1)} %all-gather.3.cloned.1.call-done, bf16[64,4,128]{2,0,1:T(8,128)(2,1)S(1)} %bitcast.355, ...), kind=kOutput, calls=%fused_computation.87 | convolution fusion | flops 336985984 | bytes 6685192 | tf_op jit(solution)/shard_map/transpose(jvp())/dot_general | solution.py:21
  142.4 3.7 %fusion.42 = bf16[8,8,8,128]{3,1,2,0:T(8,128)(2,1)S(1)} fusion(bf16[1,2560,1024]{2,1,0:T(8,128)(2,1)} %all-gather.3.cloned.1.call-done, f32[64]{0:T(128)S(1)} %fusion.149, bf16[1,2,64,2560]{3,2,1,0:T(8,128)(2,1)S(1)} %copy-done.2, s32[]{:T(128)S(6)} %select_n.66), kind=kOutput, calls=%fused_computation.28 | convolution fusion | flops 336101376 | bytes 5702148 | tf_op jit(solution)/shard_map/jvp()/dot_general | solution.py:21
  146.2 0.9 fusion.98
  147.1 1.6 convolution_convert_fusion.1
  148.9 0.2 fusion.127
  149.1 0.6 multiply_divide_fusion
  149.7 61.4 %all-reduce.13.cloned.1.call-done = (bf16[64,2560]{1,0:T(8,128)(2,1)}, bf16[64,2560]{1,0:T(8,128)(2,1)}) async-done(((bf16[64,2560]{1,0:T(8,128)(2,1)}, bf16[64,2560]{1,0:T(8,128)(2,1)}), (bf16[64,2560]{1,0:T(8,128)(2,1)}, bf16[64,2560]{1,0:T(8,128)(2,1)})) %all-reduce.13.cloned.1.call-update) | async-done | bytes 655376 | tf_op jit(solution)/shard_map/psum | solution.py:63
  211.2 1.2 add_convert_fusion.1
  212.4 9.2 %collective-permute-start.3 = (bf16[64,2560]{1,0:T(8,128)(2,1)S(1)}, bf16[64,2560]{1,0:T(8,128)(2,1)S(1)}, u32[]{:S(2)}, u32[]{:S(2)}) collective-permute-start(bf16[64,2560]{1,0:T(8,128)(2,1)S(1)} %add_convert_fusion.1), channel_id=1, source_target_pairs={{32,0},{64,32},{96,64},{128,96},{160,128},{192,160},{224,192},{256... | collective-permute-start | bytes 983048 | tf_op jit(solution)/shard_map/ppermute | solution.py:12
  221.6 1.1 fusion.94
  222.6 1.9 collective-permute-start.1
  224.6 5.2 %collective-permute-done.3 = bf16[64,2560]{1,0:T(8,128)(2,1)S(1)} collective-permute-done((bf16[64,2560]{1,0:T(8,128)(2,1)S(1)}, bf16[64,2560]{1,0:T(8,128)(2,1)S(1)}, u32[]{:S(2)}, u32[]{:S(2)}) %collective-permute-start.3) | collective-permute-done | bytes 327712 | tf_op jit(solution)/shard_map/ppermute | solution.py:12
  229.7 0.7 copy-done.4
  230.5 2.3 fusion.65
  232.8 0.9 multiply_reduce_fusion
  233.7 1.1 fusion.78
  234.8 0.9 fusion.76
  235.7 1.1 convolution_convert_fusion.6
  236.8 6.4 %collective-permute-done.1 = bf16[64,2560]{1,0:T(8,128)(2,1)S(1)} collective-permute-done((bf16[64,2560]{1,0:T(8,128)(2,1)S(1)}, bf16[64,2560]{1,0:T(8,128)(2,1)S(1)}, u32[]{:S(2)}, u32[]{:S(2)}) %collective-permute-start.1) | collective-permute-done | bytes 327712 | tf_op jit(solution)/shard_map/ppermute | solution.py:12
  243.2 1.2 fusion.95
  244.4 3.6 %fusion.48 = bf16[8,8,8,128]{3,1,2,0:T(8,128)(2,1)S(1)} fusion(bf16[1,2560,1024]{2,1,0:T(8,128)(2,1)} %all-gather.3.cloned.1.call-done, bf16[64,2560]{1,0:T(8,128)(2,1)S(1)} %get-tuple-element.9, f32[64]{0:T(128)S(1)} %add_rsqrt_fusion), kind=kOutput, calls=%fused_computation.30 | convolution fusion | flops 336101376 | bytes 5701888 | tf_op jit(solution)/shard_map/dot_general | solution.py:21
  248.1 1.8 fusion.90
  250.2 0.2 fusion.71
  250.5 0.9 fusion.99
  251.4 3.4 %convolution_convert_fusion = bf16[64,2560]{1,0:T(8,128)(2,1)} fusion(bf16[64,512]{1,0:T(8,128)(2,1)S(1)} %reshape.159, bf16[1,2560,512]{2,1,0:T(8,128)(2,1)} %all-gather.5.cloned.1.call-done), kind=kOutput, calls=%fused_computation.16 | convolution fusion | flops 167936000 | bytes 3014656 | tf_op jit(solution)/shard_map/dot_general | solution.py:34
  254.8 52.3 %all-reduce.11.cloned.1.call-done = (bf16[64,2560]{1,0:T(8,128)(2,1)}, bf16[64,2560]{1,0:T(8,128)(2,1)}) async-done(((bf16[64,2560]{1,0:T(8,128)(2,1)}, bf16[64,2560]{1,0:T(8,128)(2,1)}), (bf16[64,2560]{1,0:T(8,128)(2,1)}, bf16[64,2560]{1,0:T(8,128)(2,1)})) %all-reduce.11.cloned.1.call-update) | async-done | bytes 655376 | tf_op jit(solution)/shard_map/psum | solution.py:63
  307.2 1.8 fusion.101
  308.9 1.8 fusion.100
  (72 shorter events, 2.1 us)
Async XLA Ops:
  7.2 123.8 %copy-start.2 = (bf16[1,2,64,2560]{3,2,1,0:T(8,128)(2,1)S(1)}, bf16[1,2,64,2560]{3,2,1,0:T(8,128)(2,1)}, u32[]{:S(2)}) copy-start(bf16[1,2,64,2560]{3,2,1,0:T(8,128)(2,1)} %param.11) | copy-start | bytes 1966084
  7.2 54.8 %all-gather.5.cloned.1.call-start = ((), (), s32[]{:S(2)}) async-start(), calls=%async_computation.1 | async-start | bytes 2949120 | tf_op jit(solution)/shard_map/all_gather | solution.py:51
  7.9 123.1 %all-gather.3.cloned.1.call-start = ((), (), s32[]{:S(2)}) async-start(), calls=%async_computation | async-start | bytes 5898240 | tf_op jit(solution)/shard_map/all_gather | solution.py:50
  8.7 202.5 %all-reduce.13.cloned.1.call-start = ((), (), s32[]{:S(2)}) async-start(), calls=%async_computation.3 | async-start | bytes 1310720 | tf_op jit(solution)/shard_map/psum | solution.py:63
  8.7 29.9 %collective-permute-start = (bf16[64,2560]{1,0:T(8,128)(2,1)}, bf16[64,2560]{1,0:T(8,128)(2,1)S(1)}, u32[]{:S(2)}, u32[]{:S(2)}) collective-permute-start(bf16[64,2560]{1,0:T(8,128)(2,1)} %bitcast.364), channel_id=1, source_target_pairs={{0,32},{32,64},{64,96},{96,128},{128,160},{160,192},{192,224},{224... | collective-permute-start | bytes 983048 | tf_op jit(solution)/shard_map/ppermute | solution.py:12
  13.0 26.8 %collective-permute-start.2 = (bf16[64,2560]{1,0:T(8,128)(2,1)}, bf16[64,2560]{1,0:T(8,128)(2,1)S(1)}, u32[]{:S(2)}, u32[]{:S(2)}) collective-permute-start(bf16[64,2560]{1,0:T(8,128)(2,1)} %bitcast.365), channel_id=1, source_target_pairs={{32,0},{64,32},{96,64},{128,96},{160,128},{192,160},{224,192},{256... | collective-permute-start | bytes 983048 | tf_op jit(solution)/shard_map/ppermute | solution.py:12
  131.0 4.0 %copy-start = (bf16[1,2560,1024]{2,1,0:T(8,128)(2,1)S(1)}, bf16[1,2560,1024]{2,1,0:T(8,128)(2,1)}, u32[]{:S(2)}) copy-start(bf16[1,2560,1024]{2,1,0:T(8,128)(2,1)} %all-gather.3.cloned.1.call-done) | copy-start | bytes 15728644
  142.3 6.4 %copy-start.10 = (f32[64]{0:T(128)}, f32[64]{0:T(128)S(1)}, u32[]{:S(2)}) copy-start(f32[64]{0:T(128)S(1)} %get-tuple-element.3) | copy-start | bytes 772
  142.3 4.8 %copy-start.1 = (bf16[1,2560,512]{2,1,0:T(8,128)(2,1)S(1)}, bf16[1,2560,512]{2,1,0:T(8,128)(2,1)}, u32[]{:S(2)}) copy-start(bf16[1,2560,512]{2,1,0:T(8,128)(2,1)} %all-gather.5.cloned.1.call-done) | copy-start | bytes 7864324
  142.3 6.4 %copy-start.7 = (f32[64]{0:T(128)}, f32[64]{0:T(128)S(1)}, u32[]{:S(2)}) copy-start(f32[64]{0:T(128)S(1)} %fusion.149) | copy-start | bytes 772
  142.4 68.8 %copy-start.3 = (bf16[2,64,2560]{2,1,0:T(8,128)(2,1)S(1)}, bf16[2,64,2560]{2,1,0:T(8,128)(2,1)}, u32[]{:S(2)}) copy-start(bf16[2,64,2560]{2,1,0:T(8,128)(2,1)} %param.13) | copy-start | bytes 1966084
  146.2 75.4 %copy-start.6 = (bf16[64,4,128]{2,0,1:T(8,128)(2,1)}, bf16[64,4,128]{2,0,1:T(8,128)(2,1)S(1)}, u32[]{:S(2)}) copy-start(bf16[64,4,128]{2,0,1:T(8,128)(2,1)S(1)} %copy.51) | copy-start | bytes 196612
  148.8 158.4 %all-reduce.11.cloned.1.call-start = ((), (), s32[]{:S(2)}) async-start(), calls=%async_computation.2 | async-start | bytes 1310720 | tf_op jit(solution)/shard_map/psum | solution.py:63
  149.1 72.5 %copy-start.9 = (f32[2,2,64]{2,1,0:T(2,128)}, f32[2,2,64]{2,1,0:T(2,128)S(1)}, u32[]{:S(2)}) copy-start(f32[2,2,64]{2,1,0:T(2,128)S(1)} %get-tuple-element.35) | copy-start | bytes 3076
  211.2 36.9 %slice-start = ((s8[5242880]{0:T(1024)(128)(4,1)}), s8[1048576]{0:T(1024)(128)(4,1)S(1)}, s32[]{:S(2)}) async-start(s8[5242880]{0:T(1024)(128)(4,1)} %bitcast.342), calls=%async_computation.4 | async-start | bytes 2097152
  212.4 17.4 %collective-permute-start.3 = (bf16[64,2560]{1,0:T(8,128)(2,1)S(1)}, bf16[64,2560]{1,0:T(8,128)(2,1)S(1)}, u32[]{:S(2)}, u32[]{:S(2)}) collective-permute-start(bf16[64,2560]{1,0:T(8,128)(2,1)S(1)} %add_convert_fusion.1), channel_id=1, source_target_pairs={{32,0},{64,32},{96,64},{128,96},{160,128},{192,160},{224,192},{256... | collective-permute-start | bytes 983048 | tf_op jit(solution)/shard_map/ppermute | solution.py:12
  222.6 20.5 %collective-permute-start.1 = (bf16[64,2560]{1,0:T(8,128)(2,1)S(1)}, bf16[64,2560]{1,0:T(8,128)(2,1)S(1)}, u32[]{:S(2)}, u32[]{:S(2)}) collective-permute-start(bf16[64,2560]{1,0:T(8,128)(2,1)S(1)} %fusion.94), channel_id=1, source_target_pairs={{0,32},{32,64},{64,96},{96,128},{128,160},{160,192},{192,224},{224... | collective-permute-start | bytes 983048 | tf_op jit(solution)/shard_map/ppermute | solution.py:12
  229.7 0.7 copy-start.4
  235.7 12.4 %slice-start.1 = ((s8[5242880]{0:T(1024)(128)(4,1)}), s8[4194304]{0:T(1024)(128)(4,1)S(1)}, s32[]{:S(2)}) async-start(s8[5242880]{0:T(1024)(128)(4,1)} %bitcast.342), calls=%async_computation.5 | async-start | bytes 8388608
  244.4 5.6 %copy-start.11 = (f32[64]{0:T(128)S(1)}, f32[64]{0:T(128)}, u32[]{:S(2)}) copy-start(f32[64]{0:T(128)} %copy-done.10) | copy-start | bytes 772
  247.9 2.6 copy-start.8
  249.9 59.0 %copy-start.5 = (bf16[64,2560]{1,0:T(8,128)(2,1)S(1)}, bf16[64,2560]{1,0:T(8,128)(2,1)}, u32[]{:S(2)}) copy-start(bf16[64,2560]{1,0:T(8,128)(2,1)} %copy-done.4) | copy-start | bytes 983044
Sparse Core Ops, SparseCore 0:
  10.4 51.5 all-gather.4
  64.3 66.6 all-gather.2
  148.9 62.2 all-reduce.12
  255.0 52.1 all-reduce.10
where the time goes:
time: 319 us; the launch traced here: 317 us
  waiting for transfers between devices  218 us (68%)
  matrix products  34 us (11%)
  starting transfers between devices  30 us (9%)
  between operations  18.2 us (6%)
  other arithmetic  12.6 us (4%)
  local copies, waits for them, and re-layouts  4.07 us (1%)
    psum x2, waiting for transfers between devices, layer_forward(): lax.psum(group_partial(x, wq_local, wo_local, frames).astype(jnp.bfloat16...  114 us
    all_gather x1, waiting for transfers between devices, body(): lax.all_gather(qkv_weight, 'fsdp', axis=1, tiled=True)  66.6 us
    ppermute x4, starting transfers between devices, passed_along(): lax.ppermute(value, axis, [(source, source + steps) for source in range(i...  29.9 us
    all_gather x1, waiting for transfers between devices, body(): lax.all_gather(out_weight, 'fsdp', axis=1, tiled=True)  22.1 us
    dot_general x6, matrix products, group_partial(): jnp.dot(normed, wq, preferred_element_type=jnp.float32).astype(jnp.bfloat16)  18.2 us
    ppermute x4, waiting for transfers between devices, passed_along(): lax.ppermute(value, axis, [(source, source + steps) for source in range(i...  14.5 us
    dot_general x4, matrix products, group_partial(): lax.dot_general(context, wo, (((1,), (1,)), ((), ())), preferred_element_...  9.75 us
  transfers between devices with their start and end apart: 8, of which 7 were waited for; matrix products, arithmetic and copies ran while one was open for 5% of the time, Pallas kernels for 0%

commit v1 on v0

v1 whole, which is shorter than its diff:
```python
import jax
import jax.numpy as jnp
from jax import lax
from jax.experimental import pallas as pl
from jax.experimental.pallas import tpu as pltpu
from jax.sharding import PartitionSpec as P

HS = 128
MESH = pl.DeviceIdType.MESH
BF = jnp.bfloat16
F32 = jnp.float32
PARTS = 2
WIDE = 512


def nn(a, b):
    return jnp.dot(a, b, preferred_element_type=F32)


def nt(a, b):
    return lax.dot_general(a, b, (((1,), (1,)), ((), ())), preferred_element_type=F32)


def tn(a, b):
    return lax.dot_general(a, b, (((0,), (0,)), ((), ())), preferred_element_type=F32)


def kernel(
    fresh, sent, stash, returned, loss, plan, frames, wq, wo, out_f, out_b,
    WQ, WO, X1, X2, ST, SB, G1, G2, XN, RN, MX, PR, CT, DC, DM, PP, RB, HOP, SL, own_sem, line_send, line_recv,
    sib_send, sib_recv, loc_sem, hop_send, hop_recv, ag_send, ag_recv, rs_send, rs_recv,
):
    s = lax.axis_index("section")
    f = lax.axis_index("fsdp")
    t = lax.axis_index("tensor")
    ns, nt_ = lax.axis_size("section"), lax.axis_size("tensor")
    ny = lax.axis_size("fsdp") // 2
    y, core = f // 2, lax.rem(f, 2)
    sibling = 2 * y + 1 - core
    rows, width = X1.shape
    cut = rows // nt_
    depth = wq.shape[1]
    piece = depth // PARTS
    qh = WO.shape[1] // HS
    kh = (WQ.shape[1] // HS - qh) // 2
    group = qh // kh
    scale = HS**-0.5
    first, last = s == 0, s == ns - 1
    mine = pl.ds(pl.multiple_of(t * cut, cut), cut)

    def remote(src, dst, ss, rs, **where):
        return pltpu.make_async_remote_copy(
            src_ref=src, dst_ref=dst, send_sem=ss, recv_sem=rs, device_id=where, device_id_type=MESH
        )

    barrier = pltpu.get_barrier_semaphore()

    def greet(**where):
        pl.semaphore_signal(barrier, inc=1, device_id=where, device_id_type=MESH)

    greet(fsdp=sibling)
    for k in range(1, nt_):
        greet(tensor=lax.rem(t + k, nt_))
    pl.when(y > 0)(lambda: greet(fsdp=f - 2))
    pl.when(y < ny - 1)(lambda: greet(fsdp=f + 2))
    pl.when(s > 0)(lambda: greet(section=s - 1))
    pl.when(s < ns - 1)(lambda: greet(section=s + 1))
    partners = nt_ + jnp.where(y > 0, 1, 0) + jnp.where(y < ny - 1, 1, 0)
    partners = partners + jnp.where(s > 0, 1, 0) + jnp.where(s < ns - 1, 1, 0)
    pl.semaphore_wait(barrier, partners)

    def home(block, n):
        here, there = (wq, WQ) if n < PARTS else (wo, WO)
        at = (n % PARTS) * piece
        row = pl.multiple_of((2 * block + core) * depth + at, 16)
        return here.at[0, pl.ds(at, piece)], there.at[pl.ds(row, piece)]

    def far(block, n):
        there = WQ if n < PARTS else WO
        row = pl.multiple_of((2 * block + 1 - core) * depth + (n % PARTS) * piece, 16)
        return there.at[pl.ds(row, piece)]

    def own_sends(n):
        here, there = home(y, n)
        up = remote(here, there, own_sem.at[0, n], line_recv.at[0, 0, n], fsdp=jnp.minimum(f + 2, 2 * ny - 1))
        down = remote(here, there, own_sem.at[1, n], line_recv.at[1, 0, n], fsdp=jnp.maximum(f - 2, 0))
        over = remote(here, there, own_sem.at[2, n], sib_recv.at[0, ny - 1, n], fsdp=sibling)
        return up, down, over

    def start_own(n):
        up, down, over = own_sends(n)
        pl.when(y < ny - 1)(lambda: up.start())
        pl.when(y > 0)(lambda: down.start())
        over.start()

    def finish_own(n):
        up, down, over = own_sends(n)
        pl.when(y < ny - 1)(lambda: up.wait_send())
        pl.when(y > 0)(lambda: down.wait_send())
        over.wait_send()

    def line(d, j, n):
        block = y - 1 - j if d == 0 else y + 1 + j
        valid = block >= 0 if d == 0 else block <= ny - 1
        goes_on = jnp.logical_and(valid, y < ny - 1 if d == 0 else y > 0)
        block = jnp.clip(block, 0, ny - 1)
        there = home(block, n)[1]
        onward = jnp.clip(f + (2 if d == 0 else -2), 0, 2 * ny - 1)
        nxt = None
        if j < ny - 2:
            nxt = remote(there, there, line_send.at[d, j, n], line_recv.at[d, j + 1, n], fsdp=onward)
        got = remote(there, there, line_send.at[d, j, n], line_recv.at[d, j, n], fsdp=sibling)
        over = remote(there, there, sib_send.at[d, j, n], sib_recv.at[d, j, n], fsdp=sibling)
        other = far(block, n)
        sib = remote(other, other, sib_send.at[d, j, n], sib_recv.at[d, j, n], fsdp=sibling)
        return valid, goes_on, got, nxt, over, sib

    def relay(j, n):
        for d in range(2):
            valid, goes_on, got, nxt, over, _ = line(d, j, n)

            @pl.when(valid)
            def _():
                got.wait_recv()

            if nxt is not None:
                pl.when(goes_on)(lambda: nxt.start())
            pl.when(valid)(lambda: over.start())

    def finish_line(j, n):
        for d in range(2):
            valid, goes_on, _, nxt, over, _ = line(d, j, n)
            if nxt is not None:
                pl.when(goes_on)(lambda: nxt.wait_send())
            pl.when(valid)(lambda: over.wait_send())

    def from_sibling(n):
        other = far(y, n)
        remote(other, other, own_sem.at[2, n], sib_recv.at[0, ny - 1, n], fsdp=sibling).wait_recv()
        for j in range(ny - 1):
            for d in range(2):
                valid, _, _, _, _, sib = line(d, j, n)
                pl.when(valid)(lambda: sib.wait_recv())

    for n in range(PARTS):
        start_own(n)

    own_q = pltpu.make_async_copy(wq.at[0], WQ.at[pl.ds(pl.multiple_of(f * depth, 16), depth)], loc_sem.at[0])
    own_o = pltpu.make_async_copy(wo.at[0], WO.at[pl.ds(pl.multiple_of(f * depth, 16), depth)], loc_sem.at[1])
    saved = pltpu.make_async_copy(stash.at[0], ST, loc_sem.at[2])
    saved.start()
    own_q.start()
    own_o.start()

    def hop_down(i, src):
        return remote(src, HOP.at[i], hop_send.at[i], hop_recv.at[i], section=jnp.minimum(s + 1, ns - 1))

    def hop_up(i, src):
        return remote(src, HOP.at[i], hop_send.at[i], hop_recv.at[i], section=jnp.maximum(s - 1, 0))

    sent_hop = hop_down(0, sent.at[0, mine])
    ret_hop = hop_up(2, returned.at[0, mine])
    pl.when(s < ns - 1)(lambda: sent_hop.start())
    pl.when(s > 0)(lambda: ret_hop.start())
    fresh_in = [
        pltpu.make_async_copy(fresh.at[0], X1, loc_sem.at[3]), pltpu.make_async_copy(fresh.at[1], X2, loc_sem.at[4])
    ]
    loss_in = [
        pltpu.make_async_copy(loss.at[0], G1, loc_sem.at[5]), pltpu.make_async_copy(loss.at[1], G2, loc_sem.at[6])
    ]

    @pl.when(first)
    def _():
        for c in fresh_in:
            c.start()

    @pl.when(last)
    def _():
        for c in loss_in:
            c.start()

    far_first = sorted(range(1, nt_), key=lambda k: -min(k, nt_ - k))

    def spread(i, src, dst_at):
        return [
            remote(src, dst_at, ag_send.at[i, k - 1], ag_recv.at[i, k - 1], tensor=lax.rem(t + k, nt_)) for k in far_first
        ]

    def spread_in(i, dst):
        return [
            remote(at, at, ag_send.at[i, k - 1], ag_recv.at[i, k - 1], tensor=lax.rem(t + k, nt_))
            for k in far_first
            for at in (dst.at[pl.ds(pl.multiple_of(lax.rem(t + nt_ - k, nt_) * cut, cut), cut)],)
        ]

    def gather_start(i, got, dst):
        got.wait_recv()
        for c in spread(i, HOP.at[i], dst.at[mine]):
            c.start()
        dst[mine, :] = HOP[i]

    def gather_finish(i, dst):
        for c in spread_in(i, dst):
            c.wait_recv()
        for c in spread(i, HOP.at[i], dst.at[mine]):
            c.wait_send()

    def norm(x):
        xf = x.astype(F32)
        r = lax.rsqrt(jnp.mean(xf * xf, -1, keepdims=True) + 1e-05)
        return (xf * r).astype(BF), r

    def allowed(fr):
        fr = jnp.broadcast_to(fr, (rows, rows))
        ok = jnp.where(fr <= fr.T, 1.0, 0.0)
        return jnp.concatenate([ok] * group, axis=0) > 0.5

    def chosen(tick, a, b):
        w = plan[0, tick].astype(F32)
        return a.astype(F32) * (1.0 - w) + b.astype(F32) * w

    fr_in = frames[...].astype(F32)

    def project(m0, m1, x):
        def block(i, carry):
            cols = pl.ds(pl.multiple_of(i * WIDE, 128), WIDE)
            MX[m0:m1, cols] = nn(x[...], WQ[:, cols]).astype(BF)
            return carry

        lax.fori_loop(0, WQ.shape[1] // WIDE, block, 0)

    def heads(ref, m0, first_head):
        return jnp.concatenate(
            [ref[m0 : m0 + rows, (first_head + g) * HS : (first_head + g + 1) * HS] for g in range(group)], axis=0
        )

    def probs(m0, k, ok):
        q = heads(MX, m0, k * group)
        key = MX[m0 : m0 + rows, (qh + k) * HS : (qh + k + 1) * HS]
        w = jnp.where(ok, jnp.exp(nt(q, key) * scale), 0.0)
        return w / jnp.sum(w, -1, keepdims=True)

    def attend(m0, ok):
        for k in range(kh):
            p = probs(m0, k, ok).astype(BF)
            ctx = nn(p, MX[m0 : m0 + rows, (qh + kh + k) * HS : (qh + kh + k + 1) * HS]).astype(BF)
            for g in range(group):
                CT[:, (k * group + g) * HS : (k * group + g + 1) * HS] = ctx[g * rows : (g + 1) * rows]

    def send_out(i):
        return [
            remote(
                PP.at[i, pl.ds(pl.multiple_of(lax.rem(t + k, nt_) * cut, cut), cut)], RB.at[i, k - 1],
                rs_send.at[i, k - 1], rs_recv.at[i, k - 1], tensor=lax.rem(t + k, nt_),
            )
            for k in far_first
        ]

    def output(i):
        def block(j, carry):
            cols = pl.ds(pl.multiple_of(j * WIDE, 128), WIDE)
            PP[i, :, cols] = nt(CT[...], WO[cols, :]).astype(BF)
            return carry

        lax.fori_loop(0, width // WIDE, block, 0)
        for c in send_out(i):
            c.start()

    def reduced(i, base):
        for c in send_out(i):
            c.wait_recv()
        total = PP[i, mine, :].astype(F32)
        for k in range(1, nt_):
            total = total + RB[i, k - 1].astype(F32)
        SL[i] = (base[mine, :].astype(F32) + total).astype(BF)

    def backward(i, tick, grad):
        m0 = (1 + tick) * rows
        DC[...] = nn(grad[...], WO[...]).astype(BF)
        dots = jnp.zeros((rows, 1), F32)
        for k in range(kh):
            value = MX[m0 : m0 + rows, (qh + kh + k) * HS : (qh + kh + k + 1) * HS]
            key = MX[m0 : m0 + rows, (qh + k) * HS : (qh + k + 1) * HS]
            q = heads(MX, m0, k * group)
            dctx = heads(DC, 0, k * group)
            p = PR[tick, k]
            dp = nt(dctx, value).astype(BF).astype(F32)
            ds = (p * (dp - jnp.sum(dp * p, -1, keepdims=True)) * scale).astype(BF)
            dq = nn(ds, key).astype(BF)
            dk = tn(ds, q).astype(BF)
            dv = tn(p.astype(BF), dctx).astype(BF)
            for g in range(group):
                DM[:, (k * group + g) * HS : (k * group + g + 1) * HS] = dq[g * rows : (g + 1) * rows]
            DM[:, (qh + k) * HS : (qh + k + 1) * HS] = dk
            DM[:, (qh + kh + k) * HS : (qh + kh + k + 1) * HS] = dv
        mean = jnp.sum(DM[...].astype(F32) * MX[m0 : m0 + rows, :].astype(F32), -1, keepdims=True) / width
        r = RN[tick][:, 0:1]

        def block(j, carry):
            cols = pl.ds(pl.multiple_of(j * WIDE, 128), WIDE)
            dn = nt(DM[...], WQ[cols, :]).astype(BF).astype(F32)
            xn = SB[tick, :, cols].astype(F32) * r
            PP[i, :, cols] = (r * (dn - xn * mean)).astype(BF)
            return carry

        lax.fori_loop(0, width // WIDE, block, 0)
        for c in send_out(i):
            c.start()

    saved.wait()
    for tick in range(2):
        x = chosen(tick, ST[0], ST[1]).astype(BF)
        SB[tick] = x
        xn, r = norm(x)
        XN[(1 + tick) * rows : (2 + tick) * rows, :] = xn
        RN[tick] = jnp.broadcast_to(r, (rows, HS))
    for n in range(PARTS):
        relay(0, n)
    for n in range(PARTS, 2 * PARTS):
        start_own(n)
    pl.when(s > 0)(lambda: gather_start(0, sent_hop, X1))
    pl.when(s < ns - 1)(lambda: gather_start(2, ret_hop, G1))
    for j in range(1, ny - 1):
        for n in range(PARTS):
            relay(j, n)
    pl.when(s > 0)(lambda: gather_finish(0, X1))
    pl.when(s < ns - 1)(lambda: gather_finish(2, G1))

    @pl.when(first)
    def _():
        for c in fresh_in:
            c.wait()

    @pl.when(last)
    def _():
        for c in loss_in:
            c.wait()

    XN[0:rows, :] = norm(X1[...])[0]
    between = jnp.logical_and(y > 0, y < ny - 1)

    def relay_out():
        for j in range(ny - 1):
            for n in range(PARTS, 2 * PARTS):
                relay(j, n)

    pl.when(between)(relay_out)
    own_q.wait()
    for n in range(PARTS):
        from_sibling(n)
    project(0, 3 * rows, XN)
    attend(0, allowed(fr_in[0:1]))
    for tick in range(2):
        ok = allowed(chosen(tick, fr_in[0:1], fr_in[1:2]))
        for k in range(kh):
            PR[tick, k] = probs((1 + tick) * rows, k, ok)
    pl.when(jnp.logical_not(between))(relay_out)
    own_o.wait()
    for n in range(PARTS, 2 * PARTS):
        from_sibling(n)

    output(0)
    backward(2, 0, G1)
    reduced(0, X1)
    down = hop_down(1, SL.at[0])
    pl.when(s < ns - 1)(lambda: down.start())
    reduced(2, G1)
    up = hop_up(3, SL.at[2])
    pl.when(s > 0)(lambda: up.start())

    pl.when(s > 0)(lambda: gather_start(1, down, X2))
    pl.when(s < ns - 1)(lambda: gather_start(3, up, G2))
    pl.when(s > 0)(lambda: gather_finish(1, X2))
    XN[0:rows, :] = norm(X2[...])[0]
    project(0, rows, XN.at[0:rows])
    attend(0, allowed(fr_in[1:2]))
    output(1)
    pl.when(s < ns - 1)(lambda: gather_finish(3, G2))
    backward(3, 1, G2)
    results = []
    for i, base, out, sem in ((1, X2, out_f, 7), (3, G2, out_b, 8)):
        reduced(i, base)
        keep = pltpu.make_async_copy(SL.at[i], out.at[0, mine], loc_sem.at[sem])
        copies = spread(3 + i // 2 + 1, SL.at[i], out.at[0, mine])
        for c in copies:
            c.start()
        keep.start()
        results.append((keep, copies, spread_in(3 + i // 2 + 1, out.at[0])))
    for keep, copies, arriving in results:
        for c in arriving:
            c.wait_recv()
        for c in copies:
            c.wait_send()
        keep.wait()

    for i in range(4):
        for c in send_out(i):
            c.wait_send()
    for c in (sent_hop, down):
        pl.when(s < ns - 1)(lambda: c.wait_send())
    for c in (ret_hop, up):
        pl.when(s > 0)(lambda: c.wait_send())
    for n in range(2 * PARTS):
        finish_own(n)
        for j in range(ny - 1):
            finish_line(j, n)


def body(fresh, sent, stash, returned, loss_grads, plan, frame_ids, qkv_weight, out_weight):
    nt_ = lax.axis_size("tensor")
    n_fsdp = lax.axis_size("fsdp")
    ny = n_fsdp // 2
    _, rows, width = sent.shape
    depth, columns = qkv_weight.shape[1:]
    inner = out_weight.shape[2]
    kh = (columns - inner) // (2 * HS)
    group = inner // HS // kh
    cut = rows // nt_
    dma = pltpu.SemaphoreType.DMA
    anywhere = pl.BlockSpec(memory_space=pl.ANY)
    whole = pl.BlockSpec(memory_space=pltpu.VMEM)
    act = pltpu.VMEM((rows, width), BF)
    acts = pltpu.VMEM((2, rows, width), BF)
    return pl.pallas_call(
        kernel,
        out_shape=[jax.ShapeDtypeStruct(sent.shape, BF)] * 2,
        in_specs=[anywhere] * 5 + [pl.BlockSpec(memory_space=pltpu.SMEM), whole] + [anywhere] * 2,
        out_specs=[anywhere] * 2,
        scratch_shapes=[
            pltpu.VMEM((n_fsdp * depth, columns), BF),
            pltpu.VMEM((n_fsdp * depth, inner), BF),
            act, act, acts, acts, act, act,
            pltpu.VMEM((3 * rows, width), BF),
            pltpu.VMEM((2, rows, HS), F32),
            pltpu.VMEM((3 * rows, columns), BF),
            pltpu.VMEM((2, kh, group * rows, rows), F32),
            pltpu.VMEM((rows, inner), BF),
            pltpu.VMEM((rows, inner), BF),
            pltpu.VMEM((rows, columns), BF),
            pltpu.VMEM((4, rows, width), BF),
            pltpu.VMEM((4, nt_ - 1, cut, width), BF),
            pltpu.VMEM((4, cut, width), BF),
            pltpu.VMEM((4, cut, width), BF),
            dma((3, 2 * PARTS)),
            dma((2, ny - 1, 2 * PARTS)),
            dma((2, ny - 1, 2 * PARTS)),
            dma((2, ny - 1, 2 * PARTS)),
            dma((2, ny, 2 * PARTS)),
            dma((9,)),
            dma((4,)),
            dma((4,)),
            dma((6, nt_ - 1)),
            dma((6, nt_ - 1)),
            dma((4, nt_ - 1)),
            dma((4, nt_ - 1)),
        ],
        compiler_params=pltpu.CompilerParams(
            collective_id=0, has_side_effects=True, vmem_limit_bytes=40 << 20
        ),
        name="relay",
    )(fresh, sent, stash, returned, loss_grads, plan, frame_ids, qkv_weight, out_weight)


def solution(mesh):
    placed = (
        P(None, "fsdp", None),
        P("section", "fsdp", None),
        P("section", None, "fsdp", None),
        P("section", "fsdp", None),
        P(None, "fsdp", None),
        P("section", None),
        P(None, "fsdp"),
        P("section", "fsdp", "tensor"),
        P("section", "fsdp", "tensor"),
    )
    return jax.shard_map(
        body,
        mesh=mesh,
        in_specs=placed,
        out_specs=(P("section", "fsdp", None), P("section", "fsdp", None)),
        check_vma=False,
    )
```

time: 319 us -> 133 us (0.42)
  waiting for transfers between devices: 218 us -> 0 us
  Pallas kernels: 0 us -> 122 us
  matrix products: 34 us -> 0 us
  starting transfers between devices: 30 us -> 0 us
  between operations: 18.2 us -> 0.66 us
  other arithmetic: 12.6 us -> 0 us
  local copies, waits for them, and re-layouts: 4.07 us -> 10 us
    pallas_call x0 -> x1, Pallas kernels: none -> 122 us  [body(): pl.pallas_call(kernel, out_shape=[jax.ShapeDtypeStruct(sent.shape, BF)] *...]
    psum x2 -> x0, waiting for transfers between devices: 114 us -> none  [layer_forward(): lax.psum(group_partial(x, wq_local, wo_local, frames).astype(jnp.bfloat16...]
    all_gather x2 -> x0, waiting for transfers between devices: 88.7 us -> none  [the longest x1 66.6 us: body(): lax.all_gather(qkv_weight, 'fsdp', axis=1, tiled=True)]
    dot_general x24 -> x0, matrix products: 34 us -> none  [the longest x6 18.2 us: group_partial(): jnp.dot(normed, wq, preferred_element_type=jnp.float32).astype(jnp.bfloat16)]
    ppermute x4 -> x0, starting transfers between devices: 29.9 us -> none  [passed_along(): lax.ppermute(value, axis, [(source, source + steps) for source in range(i...]
    ppermute x4 -> x0, waiting for transfers between devices: 14.5 us -> none  [passed_along(): lax.ppermute(value, axis, [(source, source + steps) for source in range(i...]
    unnamed x32 -> x20, local copies, waits for them, and re-layouts: 1.07 us -> 10 us
    convert_element_type x4 -> x0, other arithmetic: 4.07 us -> none  [the longest x2 1.83 us: group_partial(): xf = x.astype(jnp.float32)]
  transfers between devices with their start and end apart: 8 -> 0, of which waited for: 7 -> 0; matrix products, arithmetic and copies ran while one was open for 5% -> 0% of each run, Pallas kernels for 0% -> 0%
where the time goes in v1:
time: 133 us; the launch traced here: 132 us
  Pallas kernels  122 us (92%)
  local copies, waits for them, and re-layouts  10 us (8%)
    pallas_call x1, Pallas kernels, body(): pl.pallas_call(kernel, out_shape=[jax.ShapeDtypeStruct(sent.shape, BF)] *...  122 us
    unnamed x20, local copies, waits for them, and re-layouts  10 us

profile of v1, /device:TPU:56, one launch (start us, length us, event | category | flops | bytes accessed | tf_op | source)
XLA Modules:
  0.0 132.2 jit_solution(15194696645763140321)
XLA Ops:
  0.6 0.0 copy-start
  0.6 1.1 copy-done
  1.7 0.0 copy-start.1
  1.7 1.1 copy-done.1
  2.8 0.0 copy-start.2
  2.8 1.1 copy-done.2
  3.9 0.0 copy-start.3
  3.9 1.1 copy-done.3
  5.0 0.0 copy-start.4
  5.0 1.0 copy-done.4
  6.0 0.0 copy-start.5
  6.0 1.0 copy-done.5
  6.9 0.0 copy-start.6
  6.9 1.0 copy-done.6
  7.9 0.0 copy-start.7
  7.9 0.7 copy-done.7
  8.6 0.0 copy-start.8
  8.6 0.7 copy-done.8
  9.2 121.5 %relay.1 = (bf16[1,64,2560]{2,1,0:T(8,128)(2,1)S(1)}, bf16[1,64,2560]{2,1,0:T(8,128)(2,1)S(1)}) custom-call(bf16[2,64,2560]{2,1,0:T(8,128)(2,1)S(1)} %copy-done, bf16[1,64,2560]{2,1,0:T(8,128)(2,1)S(1)} %copy-done.4, bf16[1,2,64,2560]{3,2,1,0:T(8,128)(2,1)S(1)} %copy-done.1, bf16[1,64,2560]{2,1,0:T(8,128)(2,1)S(1)} %copy-done.5, ...), custom_call_target="tpu_custom_call" | custom-call | tf_op jit(solution)/shard_map/relay/pallas_call | solution.py:424
  130.8 0.7 copy.13
  131.5 0.7 copy.14
Async XLA Ops:
  0.6 1.1 copy-start
  1.7 1.1 copy-start.1
  2.8 1.1 copy-start.2
  3.9 1.1 copy-start.3
  5.0 1.0 copy-start.4
  6.0 1.0 copy-start.5
  6.9 1.0 copy-start.6
  7.9 0.7 copy-start.7
  8.6 0.7 copy-start.8

commit v2 on v1

--- a/solution.py
+++ b/solution.py
@@ -27,7 +27,7 @@
 
 def kernel(
     fresh, sent, stash, returned, loss, plan, frames, wq, wo, out_f, out_b,
-    WQ, WO, X1, X2, ST, SB, G1, G2, XN, RN, MX, PR, CT, DC, DM, PP, RB, HOP, SL, own_sem, line_send, line_recv,
+    WQ, WO, WT, X1, X2, ST, SB, G1, G2, XN, RN, MX, PR, CT, DM, DA, PP, RB, HOP, SL, own_sem, line_send, line_recv,
     sib_send, sib_recv, loc_sem, hop_send, hop_recv, ag_send, ag_recv, rs_send, rs_recv,
 ):
     s = lax.axis_index("section")
@@ -47,6 +47,10 @@
     scale = HS**-0.5
     first, last = s == 0, s == ns - 1
     mine = pl.ds(pl.multiple_of(t * cut, cut), cut)
+    wide = width // ny
+
+    def cols(b):
+        return pl.ds(pl.multiple_of(b * wide, 128), wide)
 
     def remote(src, dst, ss, rs, **where):
         return pltpu.make_async_remote_copy(
@@ -134,13 +138,14 @@
                 pl.when(goes_on)(lambda: nxt.wait_send())
             pl.when(valid)(lambda: over.wait_send())
 
-    def from_sibling(n):
+    def own_from_sibling(n):
         other = far(y, n)
         remote(other, other, own_sem.at[2, n], sib_recv.at[0, ny - 1, n], fsdp=sibling).wait_recv()
-        for j in range(ny - 1):
-            for d in range(2):
-                valid, _, _, _, _, sib = line(d, j, n)
-                pl.when(valid)(lambda: sib.wait_recv())
+
+    def from_sibling(j, n):
+        for d in range(2):
+            valid, _, _, _, _, sib = line(d, j, n)
+            pl.when(valid)(lambda: sib.wait_recv())
 
     for n in range(PARTS):
         start_own(n)
@@ -152,11 +157,15 @@
     own_q.start()
     own_o.start()
 
-    def hop_down(i, src):
-        return remote(src, HOP.at[i], hop_send.at[i], hop_recv.at[i], section=jnp.minimum(s + 1, ns - 1))
-
-    def hop_up(i, src):
-        return remote(src, HOP.at[i], hop_send.at[i], hop_recv.at[i], section=jnp.maximum(s - 1, 0))
+    everything = pl.ds(0, width)
+
+    def hop_down(i, src, b=0):
+        at = everything if i == 0 else cols(b)
+        return remote(src.at[:, at], HOP.at[i, :, at], hop_send.at[i, b], hop_recv.at[i, b], section=jnp.minimum(s + 1, ns - 1))
+
+    def hop_up(i, src, b=0):
+        at = everything if i == 2 else cols(b)
+        return remote(src.at[:, at], HOP.at[i, :, at], hop_send.at[i, b], hop_recv.at[i, b], section=jnp.maximum(s - 1, 0))
 
     sent_hop = hop_down(0, sent.at[0, mine])
     ret_hop = hop_up(2, returned.at[0, mine])
@@ -181,28 +190,35 @@
 
     far_first = sorted(range(1, nt_), key=lambda k: -min(k, nt_ - k))
 
-    def spread(i, src, dst_at):
+    def spread(i, src, dst, at, b=0):
         return [
-            remote(src, dst_at, ag_send.at[i, k - 1], ag_recv.at[i, k - 1], tensor=lax.rem(t + k, nt_)) for k in far_first
+            remote(
+                src.at[:, at], dst.at[mine, at], ag_send.at[i, k - 1, b], ag_recv.at[i, k - 1, b], tensor=lax.rem(t + k, nt_)
+            )
+            for k in far_first
         ]
 
-    def spread_in(i, dst):
-        return [
-            remote(at, at, ag_send.at[i, k - 1], ag_recv.at[i, k - 1], tensor=lax.rem(t + k, nt_))
-            for k in far_first
-            for at in (dst.at[pl.ds(pl.multiple_of(lax.rem(t + nt_ - k, nt_) * cut, cut), cut)],)
-        ]
-
-    def gather_start(i, got, dst):
+    def spread_in(i, dst, at, b=0):
+        copies = []
+        for k in far_first:
+            there = dst.at[pl.ds(pl.multiple_of(lax.rem(t + nt_ - k, nt_) * cut, cut), cut), at]
+            copies.append(
+                remote(there, there, ag_send.at[i, k - 1, b], ag_recv.at[i, k - 1, b], tensor=lax.rem(t + k, nt_))
+            )
+        return copies
+
+    def gather_start(i, got, dst, at, b=0):
         got.wait_recv()
-        for c in spread(i, HOP.at[i], dst.at[mine]):
+        for c in spread(i, HOP.at[i], dst, at, b):
             c.start()
-        dst[mine, :] = HOP[i]
-
-    def gather_finish(i, dst):
-        for c in spread_in(i, dst):
+        dst[mine, at] = HOP[i, :, at]
+
+    def gather_finish(i, dst, at, b=0):
+        for c in spread_in(i, dst, at, b):
             c.wait_recv()
-        for c in spread(i, HOP.at[i], dst.at[mine]):
+
+    def gather_sent(i, dst, at, b=0):
+        for c in spread(i, HOP.at[i], dst, at, b):
             c.wait_send()
 
     def norm(x):
@@ -247,42 +263,38 @@
             for g in range(group):
                 CT[:, (k * group + g) * HS : (k * group + g + 1) * HS] = ctx[g * rows : (g + 1) * rows]
 
-    def send_out(i):
+    def send_out(i, b):
         return [
             remote(
-                PP.at[i, pl.ds(pl.multiple_of(lax.rem(t + k, nt_) * cut, cut), cut)], RB.at[i, k - 1],
-                rs_send.at[i, k - 1], rs_recv.at[i, k - 1], tensor=lax.rem(t + k, nt_),
+                PP.at[i, pl.ds(pl.multiple_of(lax.rem(t + k, nt_) * cut, cut), cut), cols(b)],
+                RB.at[i, k - 1, :, cols(b)],
+                rs_send.at[i, k - 1, b], rs_recv.at[i, k - 1, b], tensor=lax.rem(t + k, nt_),
             )
             for k in far_first
         ]
 
-    def output(i):
-        def block(j, carry):
-            cols = pl.ds(pl.multiple_of(j * WIDE, 128), WIDE)
-            PP[i, :, cols] = nt(CT[...], WO[cols, :]).astype(BF)
-            return carry
-
-        lax.fori_loop(0, width // WIDE, block, 0)
-        for c in send_out(i):
+    def output(i, b):
+        PP[i, :, cols(b)] = nt(CT[...], WO[cols(b), :]).astype(BF)
+        for c in send_out(i, b):
             c.start()
 
-    def reduced(i, base):
-        for c in send_out(i):
+    def reduced(i, base, b):
+        for c in send_out(i, b):
             c.wait_recv()
-        total = PP[i, mine, :].astype(F32)
+        total = PP[i, mine, cols(b)].astype(F32)
         for k in range(1, nt_):
-            total = total + RB[i, k - 1].astype(F32)
-        SL[i] = (base[mine, :].astype(F32) + total).astype(BF)
-
-    def backward(i, tick, grad):
+            total = total + RB[i, k - 1, :, cols(b)].astype(F32)
+        SL[i, :, cols(b)] = (base[mine, cols(b)].astype(F32) + total).astype(BF)
+
+    def heads_back(tick, dc):
         m0 = (1 + tick) * rows
-        DC[...] = nn(grad[...], WO[...]).astype(BF)
-        dots = jnp.zeros((rows, 1), F32)
         for k in range(kh):
             value = MX[m0 : m0 + rows, (qh + kh + k) * HS : (qh + kh + k + 1) * HS]
             key = MX[m0 : m0 + rows, (qh + k) * HS : (qh + k + 1) * HS]
             q = heads(MX, m0, k * group)
-            dctx = heads(DC, 0, k * group)
+            dctx = jnp.concatenate(
+                [dc[:, (k * group + g) * HS : (k * group + g + 1) * HS] for g in range(group)], axis=0
+            )
             p = PR[tick, k]
             dp = nt(dctx, value).astype(BF).astype(F32)
             ds = (p * (dp - jnp.sum(dp * p, -1, keepdims=True)) * scale).astype(BF)
@@ -293,18 +305,14 @@
                 DM[:, (k * group + g) * HS : (k * group + g + 1) * HS] = dq[g * rows : (g + 1) * rows]
             DM[:, (qh + k) * HS : (qh + k + 1) * HS] = dk
             DM[:, (qh + kh + k) * HS : (qh + kh + k + 1) * HS] = dv
-        mean = jnp.sum(DM[...].astype(F32) * MX[m0 : m0 + rows, :].astype(F32), -1, keepdims=True) / width
+        return jnp.sum(DM[...].astype(F32) * MX[m0 : m0 + rows, :].astype(F32), -1, keepdims=True) / width
+
+    def input_back(i, tick, mean, b):
         r = RN[tick][:, 0:1]
-
-        def block(j, carry):
-            cols = pl.ds(pl.multiple_of(j * WIDE, 128), WIDE)
-            dn = nt(DM[...], WQ[cols, :]).astype(BF).astype(F32)
-            xn = SB[tick, :, cols].astype(F32) * r
-            PP[i, :, cols] = (r * (dn - xn * mean)).astype(BF)
-            return carry
-
-        lax.fori_loop(0, width // WIDE, block, 0)
-        for c in send_out(i):
+        dn = nn(DM[...], WT[:, cols(b)]).astype(BF).astype(F32)
+        xn = SB[tick, :, cols(b)].astype(F32) * r
+        PP[i, :, cols(b)] = (r * (dn - xn * mean)).astype(BF)
+        for c in send_out(i, b):
             c.start()
 
     saved.wait()
@@ -318,13 +326,13 @@
         relay(0, n)
     for n in range(PARTS, 2 * PARTS):
         start_own(n)
-    pl.when(s > 0)(lambda: gather_start(0, sent_hop, X1))
-    pl.when(s < ns - 1)(lambda: gather_start(2, ret_hop, G1))
+    pl.when(s > 0)(lambda: gather_start(0, sent_hop, X1, everything))
+    pl.when(s < ns - 1)(lambda: gather_start(2, ret_hop, G1, everything))
     for j in range(1, ny - 1):
         for n in range(PARTS):
             relay(j, n)
-    pl.when(s > 0)(lambda: gather_finish(0, X1))
-    pl.when(s < ns - 1)(lambda: gather_finish(2, G1))
+    pl.when(s > 0)(lambda: gather_finish(0, X1, everything))
+    pl.when(s < ns - 1)(lambda: gather_finish(2, G1, everything))
 
     @pl.when(first)
     def _():
@@ -339,71 +347,137 @@
     XN[0:rows, :] = norm(X1[...])[0]
     between = jnp.logical_and(y > 0, y < ny - 1)
 
-    def relay_out():
+    out_pieces = range(PARTS, 2 * PARTS)
+
+    @pl.when(between)
+    def _():
         for j in range(ny - 1):
-            for n in range(PARTS, 2 * PARTS):
+            for n in out_pieces:
                 relay(j, n)
-
-    pl.when(between)(relay_out)
+        for n in out_pieces:
+            for j in range(ny - 1):
+                from_sibling(j, n)
+
     own_q.wait()
     for n in range(PARTS):
-        from_sibling(n)
+        own_from_sibling(n)
+        for j in range(ny - 1):
+            from_sibling(j, n)
     project(0, 3 * rows, XN)
     attend(0, allowed(fr_in[0:1]))
     for tick in range(2):
         ok = allowed(chosen(tick, fr_in[0:1], fr_in[1:2]))
         for k in range(kh):
             PR[tick, k] = probs((1 + tick) * rows, k, ok)
-    pl.when(jnp.logical_not(between))(relay_out)
-    own_o.wait()
-    for n in range(PARTS, 2 * PARTS):
-        from_sibling(n)
-
-    output(0)
-    backward(2, 0, G1)
-    reduced(0, X1)
-    down = hop_down(1, SL.at[0])
-    pl.when(s < ns - 1)(lambda: down.start())
-    reduced(2, G1)
-    up = hop_up(3, SL.at[2])
-    pl.when(s > 0)(lambda: up.start())
-
-    pl.when(s > 0)(lambda: gather_start(1, down, X2))
-    pl.when(s < ns - 1)(lambda: gather_start(3, up, G2))
-    pl.when(s > 0)(lambda: gather_finish(1, X2))
-    XN[0:rows, :] = norm(X2[...])[0]
-    project(0, rows, XN.at[0:rows])
+
+    def turn(b, carry):
+        for c in range(0, wide, HS):
+            at = pl.ds(pl.multiple_of(b * wide + c, HS), HS)
+            WT[:, at] = WQ[at, :].T
+        return carry
+
+    lax.fori_loop(0, ny, turn, 0)
+
+    def block(i):
+        return jnp.where(y < ny // 2, i, ny - 1 - i)
+
+    def reduce_down(b):
+        reduced(0, X1, b)
+        pl.when(s < ns - 1)(lambda: hop_down(1, SL.at[0], b).start())
+
+    for i in range(ny):
+        if i == 0:
+            own_o.wait()
+            for n in out_pieces:
+                own_from_sibling(n)
+        else:
+
+            @pl.when(jnp.logical_not(between))
+            def _():
+                for n in out_pieces:
+                    relay(i - 1, n)
+                for n in out_pieces:
+                    from_sibling(i - 1, n)
+
+        b = block(i)
+        output(0, b)
+        part = nn(G1[:, cols(b)], WO[cols(b), :])
+        DA[...] = part if i == 0 else DA[...] + part
+        if i >= 2:
+            reduce_down(block(i - 2))
+    mean = heads_back(0, DA[...].astype(BF))
+    for b in range(ny):
+        input_back(2, 0, mean, b)
+    for i in range(ny - 2, ny):
+        reduce_down(block(i))
+
+    for i in range(ny):
+        b = block(i)
+        pl.when(s > 0)(lambda: gather_start(1, hop_down(1, SL.at[0], b), X2, cols(b), b))
+    for b in range(ny):
+        reduced(2, G1, b)
+        pl.when(s > 0)(lambda: hop_up(3, SL.at[2], b).start())
+    for b in range(ny):
+        pl.when(s < ns - 1)(lambda: gather_start(3, hop_up(3, SL.at[2], b), G2, cols(b), b))
+    squares = jnp.zeros((rows, 1), F32)
+    mixed = jnp.zeros((rows, WQ.shape[1]), F32)
+    for i in range(ny):
+        b = block(i)
+        pl.when(s > 0)(lambda: gather_finish(1, X2, cols(b), b))
+        x = X2[:, cols(b)]
+        mixed = mixed + nn(x, WQ[cols(b), :])
+        squares = squares + jnp.sum(x.astype(F32) * x.astype(F32), -1, keepdims=True)
+    MX[0:rows, :] = (mixed * lax.rsqrt(squares / width + 1e-05)).astype(BF)
     attend(0, allowed(fr_in[1:2]))
-    output(1)
-    pl.when(s < ns - 1)(lambda: gather_finish(3, G2))
-    backward(3, 1, G2)
-    results = []
-    for i, base, out, sem in ((1, X2, out_f, 7), (3, G2, out_b, 8)):
-        reduced(i, base)
-        keep = pltpu.make_async_copy(SL.at[i], out.at[0, mine], loc_sem.at[sem])
-        copies = spread(3 + i // 2 + 1, SL.at[i], out.at[0, mine])
-        for c in copies:
+    for b in range(ny):
+        output(1, b)
+    dctx = jnp.zeros((rows, qh * HS), F32)
+    for b in range(ny):
+        pl.when(s < ns - 1)(lambda: gather_finish(3, G2, cols(b), b))
+        dctx = dctx + nn(G2[:, cols(b)], WO[cols(b), :])
+    mean = heads_back(1, dctx.astype(BF))
+
+    def finished(i, ag, base, out, b):
+        reduced(i, base, b)
+        for c in spread(ag, SL.at[i], out.at[0], cols(b), b):
             c.start()
-        keep.start()
-        results.append((keep, copies, spread_in(3 + i // 2 + 1, out.at[0])))
-    for keep, copies, arriving in results:
-        for c in arriving:
-            c.wait_recv()
-        for c in copies:
-            c.wait_send()
-        keep.wait()
-
-    for i in range(4):
-        for c in send_out(i):
-            c.wait_send()
-    for c in (sent_hop, down):
-        pl.when(s < ns - 1)(lambda: c.wait_send())
-    for c in (ret_hop, up):
-        pl.when(s > 0)(lambda: c.wait_send())
+
+    for b in range(ny):
+        input_back(3, 1, mean, b)
+        if b % 2:
+            finished(1, 4, X2, out_f, b - 1)
+            finished(1, 4, X2, out_f, b)
+    keep_f = pltpu.make_async_copy(SL.at[1], out_f.at[0, mine], loc_sem.at[7])
+    keep_f.start()
+    for b in range(ny):
+        finished(3, 5, G2, out_b, b)
+    keep_b = pltpu.make_async_copy(SL.at[3], out_b.at[0, mine], loc_sem.at[8])
+    keep_b.start()
+
     for n in range(2 * PARTS):
         finish_own(n)
         for j in range(ny - 1):
             finish_line(j, n)
+    pl.when(s < ns - 1)(lambda: sent_hop.wait_send())
+    pl.when(s > 0)(lambda: ret_hop.wait_send())
+    pl.when(s > 0)(lambda: gather_sent(0, X1, everything))
+    pl.when(s < ns - 1)(lambda: gather_sent(2, G1, everything))
+    for b in range(ny):
+        for i in range(4):
+            for c in send_out(i, b):
+                c.wait_send()
+        pl.when(s < ns - 1)(lambda: hop_down(1, SL.at[0], b).wait_send())
+        pl.when(s > 0)(lambda: hop_up(3, SL.at[2], b).wait_send())
+        pl.when(s > 0)(lambda: gather_sent(1, X2, cols(b), b))
+        pl.when(s < ns - 1)(lambda: gather_sent(3, G2, cols(b), b))
+    for i, ag, out in ((1, 4, out_f), (3, 5, out_b)):
+        for b in range(ny):
+            for c in spread_in(ag, out.at[0], cols(b), b):
+                c.wait_recv()
+            for c in spread(ag, SL.at[i], out.at[0], cols(b), b):
+                c.wait_send()
+    keep_f.wait()
+    keep_b.wait()
 
 
 def body(fresh, sent, stash, returned, loss_grads, plan, frame_ids, qkv_weight, out_weight):
@@ -429,14 +503,15 @@
         scratch_shapes=[
             pltpu.VMEM((n_fsdp * depth, columns), BF),
             pltpu.VMEM((n_fsdp * depth, inner), BF),
+            pltpu.VMEM((columns, n_fsdp * depth), BF),
             act, act, acts, acts, act, act,
             pltpu.VMEM((3 * rows, width), BF),
             pltpu.VMEM((2, rows, HS), F32),
             pltpu.VMEM((3 * rows, columns), BF),
             pltpu.VMEM((2, kh, group * rows, rows), F32),
             pltpu.VMEM((rows, inner), BF),
-            pltpu.VMEM((rows, inner), BF),
             pltpu.VMEM((rows, columns), BF),
+            pltpu.VMEM((rows, inner), F32),
             pltpu.VMEM((4, rows, width), BF),
             pltpu.VMEM((4, nt_ - 1, cut, width), BF),
             pltpu.VMEM((4, cut, width), BF),
@@ -447,15 +522,15 @@
             dma((2, ny - 1, 2 * PARTS)),
             dma((2, ny, 2 * PARTS)),
             dma((9,)),
-            dma((4,)),
-            dma((4,)),
-            dma((6, nt_ - 1)),
-            dma((6, nt_ - 1)),
-            dma((4, nt_ - 1)),
-            dma((4, nt_ - 1)),
+            dma((4, ny)),
+            dma((4, ny)),
+            dma((6, nt_ - 1, ny)),
+            dma((6, nt_ - 1, ny)),
+            dma((4, nt_ - 1, ny)),
+            dma((4, nt_ - 1, ny)),
         ],
         compiler_params=pltpu.CompilerParams(
-            collective_id=0, has_side_effects=True, vmem_limit_bytes=40 << 20
+            collective_id=0, has_side_effects=True, vmem_limit_bytes=60 << 20
         ),
         name="relay",
     )(fresh, sent, stash, returned, loss_grads, plan, frame_ids, qkv_weight, out_weight)

time: 133 us -> 118 us (0.89)
  local copies, waits for them, and re-layouts: 10 us -> 2.49 us
  Pallas kernels: 122 us -> 115 us
    unnamed x20 -> x4, local copies, waits for them, and re-layouts: 10 us -> 2.49 us
    pallas_call x1, Pallas kernels: 122 us -> 115 us  [body(): pl.pallas_call(kernel, out_shape=[jax.ShapeDtypeStruct(sent.shape, BF)] *...]
where the time goes in v2:
time: 118 us
  Pallas kernels  115 us (97%)
  local copies, waits for them, and re-layouts  2.49 us (2%)
    pallas_call x1, Pallas kernels, body(): pl.pallas_call(kernel, out_shape=[jax.ShapeDtypeStruct(sent.shape, BF)] *...  115 us
    unnamed x4, local copies, waits for them, and re-layouts  2.49 us

profile of v2, /device:TPU:56, one launch (start us, length us, event | category | flops | bytes accessed | tf_op | source)
XLA Modules:
  0.0 118.0 jit_solution(8802083282142893240)
XLA Ops:
  0.6 114.8 %relay.1 = (bf16[1,64,2560]{2,1,0:T(8,128)(2,1)}, bf16[1,64,2560]{2,1,0:T(8,128)(2,1)}) custom-call(bf16[2,64,2560]{2,1,0:T(8,128)(2,1)} %fresh.1, bf16[1,64,2560]{2,1,0:T(8,128)(2,1)} %sent.1, bf16[1,2,64,2560]{3,2,1,0:T(8,128)(2,1)} %stash.1, bf16[1,64,2560]{2,1,0:T(8,128)(2,1)} %returned.1, bf16[2,64,2560]{2,1,0:T(8,128)(2,1)} %loss.1, s32[1,2]{1,0:T(1,128)} %plan.1, ...), custom_call_target="tpu_custom_call" | custom-call | tf_op jit(solution)/shard_map/relay/pallas_call | solution.py:498
  115.5 0.0 copy-start
  115.5 1.8 %copy.13 = bf16[1,64,2560]{2,1,0:T(8,128)(2,1)} copy(bf16[1,64,2560]{2,1,0:T(8,128)(2,1)} %get-tuple-element.4) | data formatting | bytes 655360
  117.3 0.0 copy-done
  117.3 0.7 copy.14
Async XLA Ops:
  115.5 1.8 %copy-start = (bf16[1,64,2560]{2,1,0:T(8,128)(2,1)S(1)}, bf16[1,64,2560]{2,1,0:T(8,128)(2,1)}, u32[]{:S(2)}) copy-start(bf16[1,64,2560]{2,1,0:T(8,128)(2,1)} %get-tuple-element.5) | copy-start | bytes 983044

commit v3 on v2

v3 whole, which is shorter than its diff:
```python
import jax
import jax.numpy as jnp
from jax import lax
from jax.experimental import pallas as pl
from jax.experimental.pallas import tpu as pltpu
from jax.sharding import PartitionSpec as P

HS = 128
MESH = pl.DeviceIdType.MESH
BF = jnp.bfloat16
F32 = jnp.float32
PARTS = 2
WIDE = 512


def nn(a, b):
    return jnp.dot(a, b, preferred_element_type=F32)


def nt(a, b):
    return lax.dot_general(a, b, (((1,), (1,)), ((), ())), preferred_element_type=F32)


def tn(a, b):
    return lax.dot_general(a, b, (((0,), (0,)), ((), ())), preferred_element_type=F32)


def kernel(
    fresh, sent, stash, returned, loss, plan, frames, wq, wo, out_f, out_b,
    WQ, WO, WT, X1, G1, S1, X2, G2, S2, ST, FG, XN, RN, MX, PR, CT, DM, DA, PP1, RB1, SL1, HOP1, PP2, RB2, SL2, HOP2,
    own_sem, line_send, line_recv, sib_send, sib_recv, loc_sem, guest_send, guest_recv, hop1_send, hop1_recv,
    hop2_send, hop2_recv, ag_send, ag_recv, rs_send, rs_recv,
):
    s = lax.axis_index("section")
    f = lax.axis_index("fsdp")
    t = lax.axis_index("tensor")
    ns, nt_ = lax.axis_size("section"), lax.axis_size("tensor")
    ny = lax.axis_size("fsdp") // 2
    y, core = f // 2, lax.rem(f, 2)
    sibling = 2 * y + 1 - core
    rows, width = X2.shape
    cut = rows // nt_
    depth = wq.shape[1]
    piece = depth // PARTS
    qh = WO.shape[1] // HS
    kh = (WQ.shape[1] // HS - qh) // 2
    group = qh // kh
    scale = HS**-0.5
    first, last = s == 0, s == ns - 1
    mine = pl.ds(pl.multiple_of(t * cut, cut), cut)
    wide = width // ny
    between = jnp.logical_and(y > 0, y < ny - 1)
    end = jnp.logical_not(between)
    partner = jnp.where(jnp.logical_xor(y < ny // 2, between), f + 2, f - 2)
    above, below = jnp.minimum(s + 1, ns - 1), jnp.maximum(s - 1, 0)

    def cols(b):
        return pl.ds(pl.multiple_of(b * wide, 128), wide)

    def remote(src, dst, ss, rs, **where):
        return pltpu.make_async_remote_copy(
            src_ref=src, dst_ref=dst, send_sem=ss, recv_sem=rs, device_id=where, device_id_type=MESH
        )

    def also(a, b):
        return jnp.logical_and(a, b)

    barrier = pltpu.get_barrier_semaphore()

    def greet(**where):
        pl.semaphore_signal(barrier, inc=1, device_id=where, device_id_type=MESH)

    greet(fsdp=sibling)
    for k in range(1, nt_):
        greet(tensor=lax.rem(t + k, nt_))
    pl.when(y > 0)(lambda: greet(fsdp=f - 2))
    pl.when(y < ny - 1)(lambda: greet(fsdp=f + 2))
    for inside, place in ((s > 0, s - 1), (s < ns - 1, s + 1)):
        pl.when(inside)(lambda: greet(section=place, fsdp=partner))
        pl.when(also(inside, between))(lambda: greet(section=place))
    neighbours = jnp.where(s > 0, 1, 0) + jnp.where(s < ns - 1, 1, 0)
    partners = nt_ + jnp.where(y > 0, 1, 0) + jnp.where(y < ny - 1, 1, 0)
    partners = partners + neighbours + neighbours * jnp.where(between, 1, 0)
    pl.semaphore_wait(barrier, partners)

    def home(block, n):
        here, there = (wq, WQ) if n < PARTS else (wo, WO)
        at = (n % PARTS) * piece
        row = pl.multiple_of((2 * block + core) * depth + at, 16)
        return here.at[0, pl.ds(at, piece)], there.at[pl.ds(row, piece)]

    def far(block, n):
        there = WQ if n < PARTS else WO
        row = pl.multiple_of((2 * block + 1 - core) * depth + (n % PARTS) * piece, 16)
        return there.at[pl.ds(row, piece)]

    def own_sends(n):
        here, there = home(y, n)
        up = remote(here, there, own_sem.at[0, n], line_recv.at[0, 0, n], fsdp=jnp.minimum(f + 2, 2 * ny - 1))
        down = remote(here, there, own_sem.at[1, n], line_recv.at[1, 0, n], fsdp=jnp.maximum(f - 2, 0))
        over = remote(here, there, own_sem.at[2, n], sib_recv.at[0, ny - 1, n], fsdp=sibling)
        return up, down, over

    def start_own(n):
        up, down, over = own_sends(n)
        pl.when(y < ny - 1)(lambda: up.start())
        pl.when(y > 0)(lambda: down.start())
        over.start()

    def finish_own(n):
        up, down, over = own_sends(n)
        pl.when(y < ny - 1)(lambda: up.wait_send())
        pl.when(y > 0)(lambda: down.wait_send())
        over.wait_send()

    def line(d, j, n):
        block = y - 1 - j if d == 0 else y + 1 + j
        valid = block >= 0 if d == 0 else block <= ny - 1
        goes_on = jnp.logical_and(valid, y < ny - 1 if d == 0 else y > 0)
        block = jnp.clip(block, 0, ny - 1)
        there = home(block, n)[1]
        onward = jnp.clip(f + (2 if d == 0 else -2), 0, 2 * ny - 1)
        nxt = None
        if j < ny - 2:
            nxt = remote(there, there, line_send.at[d, j, n], line_recv.at[d, j + 1, n], fsdp=onward)
        got = remote(there, there, line_send.at[d, j, n], line_recv.at[d, j, n], fsdp=sibling)
        over = remote(there, there, sib_send.at[d, j, n], sib_recv.at[d, j, n], fsdp=sibling)
        other = far(block, n)
        sib = remote(other, other, sib_send.at[d, j, n], sib_recv.at[d, j, n], fsdp=sibling)
        return valid, goes_on, got, nxt, over, sib

    def relay(j, n):
        for d in range(2):
            valid, goes_on, got, nxt, over, _ = line(d, j, n)

            @pl.when(valid)
            def _():
                got.wait_recv()

            if nxt is not None:
                pl.when(goes_on)(lambda: nxt.start())
            pl.when(valid)(lambda: over.start())

    def finish_line(j, n):
        for d in range(2):
            valid, goes_on, _, nxt, over, _ = line(d, j, n)
            if nxt is not None:
                pl.when(goes_on)(lambda: nxt.wait_send())
            pl.when(valid)(lambda: over.wait_send())

    def own_from_sibling(n):
        other = far(y, n)
        remote(other, other, own_sem.at[2, n], sib_recv.at[0, ny - 1, n], fsdp=sibling).wait_recv()

    def from_sibling(j, n):
        for d in range(2):
            valid, _, _, _, _, sib = line(d, j, n)
            pl.when(valid)(lambda: sib.wait_recv())

    for n in range(PARTS):
        start_own(n)

    own_q = pltpu.make_async_copy(wq.at[0], WQ.at[pl.ds(pl.multiple_of(f * depth, 16), depth)], loc_sem.at[0])
    own_o = pltpu.make_async_copy(wo.at[0], WO.at[pl.ds(pl.multiple_of(f * depth, 16), depth)], loc_sem.at[1])
    saved = pltpu.make_async_copy(stash.at[0], ST, loc_sem.at[2])
    saved.start()

    def hop1(i, g):
        src = (sent, returned)[i].at[0, mine]
        place = (above, below)[i]
        to = partner if g else f
        return remote(src, HOP1.at[i, g], hop1_send.at[i], hop1_recv.at[i, g], section=place, fsdp=to)

    goes = (s < ns - 1, s > 0)
    comes = (s > 0, s < ns - 1)
    edge = (first, last)
    for i in range(2):
        pl.when(also(goes[i], between))(lambda: hop1(i, 0).start())
        pl.when(also(goes[i], end))(lambda: hop1(i, 1).start())

    first_in = (X1, G1)
    second_in = (X2, G2)
    at_hand = (fresh, loss)
    own_in = [pltpu.make_async_copy(at_hand[i].at[0], first_in[i].at[0], loc_sem.at[3 + i]) for i in range(2)]
    own_in2 = [pltpu.make_async_copy(at_hand[i].at[1], second_in[i], loc_sem.at[5 + i]) for i in range(2)]
    guest_in = [
        remote(at_hand[i].at[0], first_in[i].at[1], guest_send.at[i], guest_recv.at[i], fsdp=partner) for i in range(2)
    ]
    guest_stash = remote(S1.at[0], S1.at[1], guest_send.at[2], guest_recv.at[2], fsdp=partner)
    guest_frames = remote(frames, FG, guest_send.at[3], guest_recv.at[3], fsdp=partner)
    for i in range(2):
        pl.when(also(edge[i], between))(lambda: own_in[i].start())
        pl.when(also(edge[i], end))(lambda: guest_in[i].start())
        pl.when(edge[i])(lambda: own_in2[i].start())
    pl.when(end)(lambda: guest_frames.start())
    own_q.start()
    own_o.start()

    far_first = sorted(range(1, nt_), key=lambda k: -min(k, nt_ - k))

    def peer(k):
        return lax.rem(t + k, nt_)

    def part_of(k):
        return pl.ds(pl.multiple_of(lax.rem(t + k, nt_) * cut, cut), cut)

    def spread1(i):
        return [
            remote(HOP1.at[i], first_in[i].at[:, mine], ag_send.at[i, k - 1, 0], ag_recv.at[i, k - 1, 0], tensor=peer(k))
            for k in far_first
        ]

    def spread1_in(i):
        copies = []
        for k in far_first:
            there = first_in[i].at[:, part_of(nt_ - k)]
            copies.append(remote(there, there, ag_send.at[i, k - 1, 0], ag_recv.at[i, k - 1, 0], tensor=peer(k)))
        return copies

    def spread(i, src, dst, b):
        at = cols(b)
        return [
            remote(src.at[:, at], dst.at[mine, at], ag_send.at[i, k - 1, b], ag_recv.at[i, k - 1, b], tensor=peer(k))
            for k in far_first
        ]

    def spread_in(i, dst, b):
        copies = []
        for k in far_first:
            there = dst.at[part_of(nt_ - k), cols(b)]
            copies.append(remote(there, there, ag_send.at[i, k - 1, b], ag_recv.at[i, k - 1, b], tensor=peer(k)))
        return copies

    def hop2(i, g, b):
        place = (above, below)[i]
        to = partner if g else f
        return remote(
            SL1.at[i, g, :, cols(b)], HOP2.at[i, :, cols(b)], hop2_send.at[i, g, b], hop2_recv.at[i, b], section=place, fsdp=to
        )

    def gather2(i, b):
        hop2(i, 0, b).wait_recv()
        for c in spread(2 + i, HOP2.at[i], second_in[i], b):
            c.start()
        second_in[i][mine, cols(b)] = HOP2[i, :, cols(b)]

    def gathered2(i, b):
        for c in spread_in(2 + i, second_in[i], b):
            c.wait_recv()

    def norm(x):
        xf = x.astype(F32)
        r = lax.rsqrt(jnp.mean(xf * xf, -1, keepdims=True) + 1e-05)
        return (xf * r).astype(BF), r

    def allowed(fr):
        fr = jnp.broadcast_to(fr, (rows, rows))
        ok = jnp.where(fr <= fr.T, 1.0, 0.0)
        return jnp.concatenate([ok] * group, axis=0) > 0.5

    def chosen(tick, a, b):
        w = plan[0, tick].astype(F32)
        return a.astype(F32) * (1.0 - w) + b.astype(F32) * w

    def project(m0, m1):
        def block(i, carry):
            at = pl.ds(pl.multiple_of(i * WIDE, 128), WIDE)
            MX[m0:m1, at] = nn(XN[m0:m1, :], WQ[:, at]).astype(BF)
            return carry

        lax.fori_loop(0, WQ.shape[1] // WIDE, block, 0)

    fw, b1, b2 = (0, rows), (2 * rows, 3 * rows), 4 * rows

    def heads(m0, first_head):
        return jnp.concatenate(
            [MX[m0 : m0 + rows, (first_head + g) * HS : (first_head + g + 1) * HS] for g in range(group)], axis=0
        )

    def probs(m0, k, ok):
        key = MX[m0 : m0 + rows, (qh + k) * HS : (qh + k + 1) * HS]
        w = jnp.where(ok, jnp.exp(nt(heads(m0, k * group), key) * scale), 0.0)
        return w / jnp.sum(w, -1, keepdims=True)

    def attend(m0, ok):
        for k in range(kh):
            p = probs(m0, k, ok).astype(BF)
            ctx = nn(p, MX[m0 : m0 + rows, (qh + kh + k) * HS : (qh + kh + k + 1) * HS]).astype(BF)
            for g in range(group):
                CT[m0 : m0 + rows, (k * group + g) * HS : (k * group + g + 1) * HS] = ctx[g * rows : (g + 1) * rows]

    def keep_probs(slot, m0, ok):
        for k in range(kh):
            PR[slot, k] = probs(m0, k, ok)

    def send1(i, b):
        return [
            remote(
                PP1.at[i, :, part_of(k), cols(b)], RB1.at[i, k - 1, :, :, cols(b)],
                rs_send.at[i, k - 1, b], rs_recv.at[i, k - 1, b], tensor=peer(k),
            )
            for k in far_first
        ]

    def send2(i, b):
        return [
            remote(
                PP2.at[i, part_of(k), cols(b)], RB2.at[i, k - 1, :, cols(b)],
                rs_send.at[2 + i, k - 1, b], rs_recv.at[2 + i, k - 1, b], tensor=peer(k),
            )
            for k in far_first
        ]

    def reduced1(i, b):
        for c in send1(i, b):
            c.wait_recv()
        for g in range(2):
            total = PP1[i, g, mine, cols(b)].astype(F32)
            for k in range(1, nt_):
                total = total + RB1[i, k - 1, g, :, cols(b)].astype(F32)
            SL1[i, g, :, cols(b)] = (first_in[i][g, mine, cols(b)].astype(F32) + total).astype(BF)
        for g in (1, 0):
            pl.when(goes[i])(lambda: hop2(i, g, b).start())

    def reduced2(i, b):
        for c in send2(i, b):
            c.wait_recv()
        total = PP2[i, mine, cols(b)].astype(F32)
        for k in range(1, nt_):
            total = total + RB2[i, k - 1, :, cols(b)].astype(F32)
        SL2[i, :, cols(b)] = (second_in[i][mine, cols(b)].astype(F32) + total).astype(BF)
        for c in spread(4 + i, SL2.at[i], (out_f, out_b)[i].at[0], b):
            c.start()

    def heads_back(slot, m0, d0, dc):
        for k in range(kh):
            value = MX[m0 : m0 + rows, (qh + kh + k) * HS : (qh + kh + k + 1) * HS]
            key = MX[m0 : m0 + rows, (qh + k) * HS : (qh + k + 1) * HS]
            q = heads(m0, k * group)
            dctx = jnp.concatenate(
                [dc[:, (k * group + g) * HS : (k * group + g + 1) * HS] for g in range(group)], axis=0
            )
            p = PR[slot, k]
            dp = nt(dctx, value).astype(BF).astype(F32)
            ds = (p * (dp - jnp.sum(dp * p, -1, keepdims=True)) * scale).astype(BF)
            dq = nn(ds, key).astype(BF)
            dk = tn(ds, q).astype(BF)
            dv = tn(p.astype(BF), dctx).astype(BF)
            for g in range(group):
                DM[d0 : d0 + rows, (k * group + g) * HS : (k * group + g + 1) * HS] = dq[g * rows : (g + 1) * rows]
            DM[d0 : d0 + rows, (qh + k) * HS : (qh + k + 1) * HS] = dk
            DM[d0 : d0 + rows, (qh + kh + k) * HS : (qh + kh + k + 1) * HS] = dv
        return (
            jnp.sum(DM[d0 : d0 + rows, :].astype(F32) * MX[m0 : m0 + rows, :].astype(F32), -1, keepdims=True) / width
        )

    def norm_back(slot, dn, x, mean):
        r = RN[slot][:, 0:1]
        return (r * (dn.astype(BF).astype(F32) - x.astype(F32) * r * mean)).astype(BF)

    def turn(b, carry):
        for c in range(0, wide, HS):
            at = pl.ds(pl.multiple_of(b * wide + c, HS), HS)
            WT[:, at] = WQ[at, :].T
        return carry

    def turn_all():
        lax.fori_loop(0, ny, turn, 0)

    in_pieces = range(PARTS)
    out_pieces = range(PARTS, 2 * PARTS)

    def prepare(slot, m0, x):
        xn, r = norm(x)
        XN[m0 : m0 + rows, :] = xn
        RN[slot] = jnp.broadcast_to(r, (rows, HS))

    saved.wait()
    S1[0] = chosen(0, ST[0], ST[1]).astype(BF)
    pl.when(end)(lambda: guest_stash.start())
    x = chosen(1, ST[0], ST[1]).astype(BF)
    S2[...] = x
    prepare(2, b2, x)
    for n in in_pieces:
        relay(0, n)
    for n in out_pieces:
        start_own(n)

    @pl.when(between)
    def _():
        for i in range(2):

            @pl.when(comes[i])
            def _():
                for g in range(2):
                    hop1(i, g).wait_recv()
                for c in spread1(i):
                    c.start()
                for g in range(2):
                    first_in[i][g, mine, :] = HOP1[i, g]

        prepare(0, b1[0], S1[0])

    for j in range(1, ny - 1):
        for n in in_pieces:
            relay(j, n)

    @pl.when(between)
    def _():
        for i in range(2):

            @pl.when(comes[i])
            def _():
                for c in spread1_in(i):
                    c.wait_recv()

            @pl.when(edge[i])
            def _():
                own_in[i].wait()
                guest_in[i].wait_recv()

        guest_stash.wait_recv()
        guest_frames.wait_recv()
        prepare(1, b1[1], S1[1])
        for g in range(2):
            XN[fw[g] : fw[g] + rows, :] = norm(X1[g])[0]

    own_q.wait()
    for n in in_pieces:
        own_from_sibling(n)
        for j in range(ny - 1):
            from_sibling(j, n)
    fr = frames[...].astype(F32)

    def keep_second():
        keep_probs(2, b2, allowed(chosen(1, fr[0:1], fr[1:2])))

    def arrive(i):
        for b in range(ny):
            pl.when(comes[i])(lambda: gather2(i, b))

    def second_forward():
        pl.when(edge[0])(lambda: own_in2[0].wait())
        squares = jnp.zeros((rows, 1), F32)
        mixed = jnp.zeros((rows, WQ.shape[1]), F32)
        for b in range(ny):
            pl.when(comes[0])(lambda: gathered2(0, b))
            x = X2[:, cols(b)]
            mixed = mixed + nn(x, WQ[cols(b), :])
            squares = squares + jnp.sum(x.astype(F32) * x.astype(F32), -1, keepdims=True)
        MX[0:rows, :] = (mixed * lax.rsqrt(squares / width + 1e-05)).astype(BF)
        attend(0, allowed(fr[1:2]))

    @pl.when(end)
    def _():
        project(b2, b2 + rows)
        keep_second()
        turn_all()
        own_o.wait()
        for n in out_pieces:
            own_from_sibling(n)
        for j in range(ny - 2):
            for n in out_pieces:
                relay(j, n)
            for n in out_pieces:
                from_sibling(j, n)
        arrive(0)
        second_forward()
        for n in out_pieces:
            relay(ny - 2, n)
        arrive(1)
        for n in out_pieces:
            from_sibling(ny - 2, n)

    @pl.when(between)
    def _():
        project(0, b2 + rows)
        guest = FG[...].astype(F32)
        marks = (fr, guest)
        for n in out_pieces:
            relay(0, n)
        for g in range(2):
            attend(fw[g], allowed(marks[g][0:1]))
        for g in range(2):
            keep_probs(g, b1[g], allowed(chosen(0, marks[g][0:1], marks[g][1:2])))
        turn_all()
        order = (1, 0, 2, 3)
        for i in range(ny):
            if i == 0:
                own_o.wait()
                for n in out_pieces:
                    own_from_sibling(n)
            elif i == 1:
                for n in out_pieces:
                    from_sibling(0, n)
            elif i == 3:
                for j in range(1, ny - 1):
                    for n in out_pieces:
                        relay(j, n)
                    for n in out_pieces:
                        from_sibling(j, n)
            b = jnp.where(y < ny // 2, order[i], ny - 1 - order[i])
            weight = WO[cols(b), :]
            part = nt(CT[...], weight).astype(BF)
            for g in range(2):
                PP1[0, g, :, cols(b)] = part[g * rows : (g + 1) * rows]
            for c in send1(0, b):
                c.start()
            grad = jnp.concatenate([G1[0, :, cols(b)], G1[1, :, cols(b)]], axis=0)
            part = nn(grad, weight)
            DA[...] = part if i == 0 else DA[...] + part
        mean = [heads_back(g, b1[g], g * rows, DA[g * rows : (g + 1) * rows, :].astype(BF)) for g in range(2)]
        for b in range(ny):
            dn = nn(DM[...], WT[:, cols(b)])
            for g in range(2):
                PP1[1, g, :, cols(b)] = norm_back(g, dn[g * rows : (g + 1) * rows], S1[g, :, cols(b)], mean[g])
            for c in send1(1, b):
                c.start()
        for b in range(ny):
            reduced1(0, b)
        for b in range(ny):
            reduced1(1, b)
        arrive(0)
        keep_second()
        arrive(1)
        second_forward()

    for b in range(ny):
        PP2[0, :, cols(b)] = nt(CT[0:rows, :], WO[cols(b), :]).astype(BF)
        for c in send2(0, b):
            c.start()
    pl.when(edge[1])(lambda: own_in2[1].wait())
    dctx = jnp.zeros((rows, qh * HS), F32)
    for b in range(ny):
        pl.when(comes[1])(lambda: gathered2(1, b))
        dctx = dctx + nn(G2[:, cols(b)], WO[cols(b), :])
    mean = heads_back(2, b2, 0, dctx.astype(BF))
    for b in range(ny):
        PP2[1, :, cols(b)] = norm_back(2, nn(DM[0:rows, :], WT[:, cols(b)]), S2[:, cols(b)], mean)
        for c in send2(1, b):
            c.start()
        if b % 2:
            reduced2(0, b - 1)
            reduced2(0, b)
    keep_f = pltpu.make_async_copy(SL2.at[0], out_f.at[0, mine], loc_sem.at[7])
    keep_f.start()
    for b in range(ny):
        reduced2(1, b)
    keep_b = pltpu.make_async_copy(SL2.at[1], out_b.at[0, mine], loc_sem.at[8])
    keep_b.start()

    for n in range(2 * PARTS):
        finish_own(n)
        for j in range(ny - 1):
            finish_line(j, n)

    @pl.when(end)
    def _():
        guest_stash.wait_send()
        guest_frames.wait_send()

    for i in range(2):
        pl.when(goes[i])(lambda: hop1(i, 0).wait_send())
        pl.when(also(edge[i], end))(lambda: guest_in[i].wait_send())

        @pl.when(between)
        def _():
            @pl.when(comes[i])
            def _():
                for c in spread1(i):
                    c.wait_send()

            for b in range(ny):
                for c in send1(i, b):
                    c.wait_send()
                for g in range(2):
                    pl.when(goes[i])(lambda: hop2(i, g, b).wait_send())

        for b in range(ny):
            for c in send2(i, b):
                c.wait_send()

            @pl.when(comes[i])
            def _():
                for c in spread(2 + i, HOP2.at[i], second_in[i], b):
                    c.wait_send()

    for i, out in ((0, out_f), (1, out_b)):
        for b in range(ny):
            for c in spread_in(4 + i, out.at[0], b):
                c.wait_recv()
            for c in spread(4 + i, SL2.at[i], out.at[0], b):
                c.wait_send()
    keep_f.wait()
    keep_b.wait()


def body(fresh, sent, stash, returned, loss_grads, plan, frame_ids, qkv_weight, out_weight):
    nt_ = lax.axis_size("tensor")
    n_fsdp = lax.axis_size("fsdp")
    ny = n_fsdp // 2
    _, rows, width = sent.shape
    depth, columns = qkv_weight.shape[1:]
    inner = out_weight.shape[2]
    kh = (columns - inner) // (2 * HS)
    group = inner // HS // kh
    cut = rows // nt_
    dma = pltpu.SemaphoreType.DMA
    anywhere = pl.BlockSpec(memory_space=pl.ANY)
    whole = pl.BlockSpec(memory_space=pltpu.VMEM)
    act = pltpu.VMEM((rows, width), BF)
    acts = pltpu.VMEM((2, rows, width), BF)
    return pl.pallas_call(
        kernel,
        out_shape=[jax.ShapeDtypeStruct(sent.shape, BF)] * 2,
        in_specs=[anywhere] * 5 + [pl.BlockSpec(memory_space=pltpu.SMEM), whole] + [anywhere] * 2,
        out_specs=[anywhere] * 2,
        scratch_shapes=[
            pltpu.VMEM((n_fsdp * depth, columns), BF),
            pltpu.VMEM((n_fsdp * depth, inner), BF),
            pltpu.VMEM((columns, n_fsdp * depth), BF),
            acts, acts, acts, act, act, act, acts,
            pltpu.VMEM(frame_ids.shape, jnp.int32),
            pltpu.VMEM((5 * rows, width), BF),
            pltpu.VMEM((3, rows, HS), F32),
            pltpu.VMEM((5 * rows, columns), BF),
            pltpu.VMEM((3, kh, group * rows, rows), F32),
            pltpu.VMEM((2 * rows, inner), BF),
            pltpu.VMEM((2 * rows, columns), BF),
            pltpu.VMEM((2 * rows, inner), F32),
            pltpu.VMEM((2, 2, rows, width), BF),
            pltpu.VMEM((2, nt_ - 1, 2, cut, width), BF),
            pltpu.VMEM((2, 2, cut, width), BF),
            pltpu.VMEM((2, 2, cut, width), BF),
            pltpu.VMEM((2, rows, width), BF),
            pltpu.VMEM((2, nt_ - 1, cut, width), BF),
            pltpu.VMEM((2, cut, width), BF),
            pltpu.VMEM((2, cut, width), BF),
            dma((3, 2 * PARTS)),
            dma((2, ny - 1, 2 * PARTS)),
            dma((2, ny - 1, 2 * PARTS)),
            dma((2, ny - 1, 2 * PARTS)),
            dma((2, ny, 2 * PARTS)),
            dma((9,)),
            dma((4,)),
            dma((4,)),
            dma((2,)),
            dma((2, 2)),
            dma((2, 2, ny)),
            dma((2, ny)),
            dma((6, nt_ - 1, ny)),
            dma((6, nt_ - 1, ny)),
            dma((4, nt_ - 1, ny)),
            dma((4, nt_ - 1, ny)),
        ],
        compiler_params=pltpu.CompilerParams(
            collective_id=0, has_side_effects=True, vmem_limit_bytes=60 << 20
        ),
        name="relay",
    )(fresh, sent, stash, returned, loss_grads, plan, frame_ids, qkv_weight, out_weight)


def solution(mesh):
    placed = (
        P(None, "fsdp", None),
        P("section", "fsdp", None),
        P("section", None, "fsdp", None),
        P("section", "fsdp", None),
        P(None, "fsdp", None),
        P("section", None),
        P(None, "fsdp"),
        P("section", "fsdp", "tensor"),
        P("section", "fsdp", "tensor"),
    )
    return jax.shard_map(
        body,
        mesh=mesh,
        in_specs=placed,
        out_specs=(P("section", "fsdp", None), P("section", "fsdp", None)),
        check_vma=False,
    )
```

time: 118 us -> 112 us (0.949)
  Pallas kernels: 115 us -> 109 us
    pallas_call x1, Pallas kernels: 115 us -> 109 us  [body(): pl.pallas_call(kernel, out_shape=[jax.ShapeDtypeStruct(sent.shape, BF)] *...]
where the time goes in v3:
time: 112 us
  Pallas kernels  109 us (97%)
  local copies, waits for them, and re-layouts  2.49 us (2%)
    pallas_call x1, Pallas kernels, body(): pl.pallas_call(kernel, out_shape=[jax.ShapeDtypeStruct(sent.shape, BF)] *...  109 us
    unnamed x4, local copies, waits for them, and re-layouts  2.49 us

profile of v3, /device:TPU:56, one launch (start us, length us, event | category | flops | bytes accessed | tf_op | source)
XLA Modules:
  0.0 112.1 jit_solution(17560505284259835839)
XLA Ops:
  0.6 108.9 %relay.1 = (bf16[1,64,2560]{2,1,0:T(8,128)(2,1)}, bf16[1,64,2560]{2,1,0:T(8,128)(2,1)}) custom-call(bf16[2,64,2560]{2,1,0:T(8,128)(2,1)} %fresh.1, bf16[1,64,2560]{2,1,0:T(8,128)(2,1)} %sent.1, bf16[1,2,64,2560]{3,2,1,0:T(8,128)(2,1)} %stash.1, bf16[1,64,2560]{2,1,0:T(8,128)(2,1)} %returned.1, bf16[2,64,2560]{2,1,0:T(8,128)(2,1)} %loss.1, s32[1,2]{1,0:T(1,128)} %plan.1, ...), custom_call_target="tpu_custom_call" | custom-call | tf_op jit(solution)/shard_map/relay/pallas_call | solution.py:613
  109.6 0.0 copy-start
  109.6 1.8 %copy.13 = bf16[1,64,2560]{2,1,0:T(8,128)(2,1)} copy(bf16[1,64,2560]{2,1,0:T(8,128)(2,1)} %get-tuple-element.4) | data formatting | bytes 655360
  111.3 0.0 copy-done
  111.3 0.7 copy.14
Async XLA Ops:
  109.6 1.8 %copy-start = (bf16[1,64,2560]{2,1,0:T(8,128)(2,1)S(1)}, bf16[1,64,2560]{2,1,0:T(8,128)(2,1)}, u32[]{:S(2)}) copy-start(bf16[1,64,2560]{2,1,0:T(8,128)(2,1)} %get-tuple-element.5) | copy-start | bytes 983044

commit v4 on v3

--- a/solution.py
+++ b/solution.py
@@ -29,7 +29,7 @@
     fresh, sent, stash, returned, loss, plan, frames, wq, wo, out_f, out_b,
     WQ, WO, WT, X1, G1, S1, X2, G2, S2, ST, FG, XN, RN, MX, PR, CT, DM, DA, PP1, RB1, SL1, HOP1, PP2, RB2, SL2, HOP2,
     own_sem, line_send, line_recv, sib_send, sib_recv, loc_sem, guest_send, guest_recv, hop1_send, hop1_recv,
-    hop2_send, hop2_recv, ag_send, ag_recv, rs_send, rs_recv,
+    hop2_send, hop2_recv, ag_send, ag_recv, rs_send, rs_recv, open_sem,
 ):
     s = lax.axis_index("section")
     f = lax.axis_index("fsdp")
@@ -52,6 +52,7 @@
     between = jnp.logical_and(y > 0, y < ny - 1)
     end = jnp.logical_not(between)
     partner = jnp.where(jnp.logical_xor(y < ny // 2, between), f + 2, f - 2)
+    wrap = s == ns // 2
     above, below = jnp.minimum(s + 1, ns - 1), jnp.maximum(s - 1, 0)
 
     def cols(b):
@@ -75,13 +76,18 @@
         greet(tensor=lax.rem(t + k, nt_))
     pl.when(y > 0)(lambda: greet(fsdp=f - 2))
     pl.when(y < ny - 1)(lambda: greet(fsdp=f + 2))
-    for inside, place in ((s > 0, s - 1), (s < ns - 1, s + 1)):
-        pl.when(inside)(lambda: greet(section=place, fsdp=partner))
-        pl.when(also(inside, between))(lambda: greet(section=place))
-    neighbours = jnp.where(s > 0, 1, 0) + jnp.where(s < ns - 1, 1, 0)
+    pl.when(s > 0)(lambda: greet(section=s - 1, fsdp=partner))
+    pl.when(also(s > 0, between))(lambda: greet(section=s - 1))
+    links = jnp.where(between, 2, 1)
     partners = nt_ + jnp.where(y > 0, 1, 0) + jnp.where(y < ny - 1, 1, 0)
-    partners = partners + neighbours + neighbours * jnp.where(between, 1, 0)
+    partners = partners + links * jnp.where(s < ns - 1, 1, 0)
     pl.semaphore_wait(barrier, partners)
+
+    def answer(**where):
+        pl.semaphore_signal(open_sem, inc=1, device_id=where, device_id_type=MESH)
+
+    pl.when(s < ns - 1)(lambda: answer(section=s + 1, fsdp=partner))
+    pl.when(also(s < ns - 1, between))(lambda: answer(section=s + 1))
 
     def home(block, n):
         here, there = (wq, WQ) if n < PARTS else (wo, WO)
@@ -174,20 +180,22 @@
     goes = (s < ns - 1, s > 0)
     comes = (s > 0, s < ns - 1)
     edge = (first, last)
-    for i in range(2):
-        pl.when(also(goes[i], between))(lambda: hop1(i, 0).start())
-        pl.when(also(goes[i], end))(lambda: hop1(i, 1).start())
-
     first_in = (X1, G1)
     second_in = (X2, G2)
     at_hand = (fresh, loss)
-    own_in = [pltpu.make_async_copy(at_hand[i].at[0], first_in[i].at[0], loc_sem.at[3 + i]) for i in range(2)]
+
+    def send_hop1(i):
+        pl.when(also(goes[i], between))(lambda: hop1(i, 0).start())
+        pl.when(also(goes[i], end))(lambda: hop1(i, 1).start())
+
+    own_in = [pltpu.make_async_copy(at_hand[i].at[0, mine], HOP1.at[i, 0], hop1_recv.at[i, 0]) for i in range(2)]
     own_in2 = [pltpu.make_async_copy(at_hand[i].at[1], second_in[i], loc_sem.at[5 + i]) for i in range(2)]
     guest_in = [
-        remote(at_hand[i].at[0], first_in[i].at[1], guest_send.at[i], guest_recv.at[i], fsdp=partner) for i in range(2)
+        remote(at_hand[i].at[0, mine], HOP1.at[i, 1], guest_send.at[i], hop1_recv.at[i, 1], fsdp=partner) for i in range(2)
     ]
-    guest_stash = remote(S1.at[0], S1.at[1], guest_send.at[2], guest_recv.at[2], fsdp=partner)
-    guest_frames = remote(frames, FG, guest_send.at[3], guest_recv.at[3], fsdp=partner)
+    guest_stash = remote(S1.at[0], S1.at[1], guest_send.at[2], guest_recv.at[0], fsdp=partner)
+    guest_frames = remote(frames, FG, guest_send.at[3], guest_recv.at[1], fsdp=partner)
+    send_hop1(0)
     for i in range(2):
         pl.when(also(edge[i], between))(lambda: own_in[i].start())
         pl.when(also(edge[i], end))(lambda: guest_in[i].start())
@@ -386,38 +394,41 @@
     for n in out_pieces:
         start_own(n)
 
+    pl.when(s > 0)(lambda: pl.semaphore_wait(open_sem, links))
+    send_hop1(1)
+
+    def arrive1(i):
+        for g in range(2):
+            hop1(i, g).wait_recv()
+        for c in spread1(i):
+            c.start()
+        for g in range(2):
+            first_in[i][g, mine, :] = HOP1[i, g]
+
+    @pl.when(between)
+    def _():
+        arrive1(0)
+        prepare(0, b1[0], S1[0])
+
+    for n in in_pieces:
+        relay(1, n)
+        if n == 0:
+            pl.when(between)(lambda: arrive1(1))
+
+    @pl.when(between)
+    def _():
+        for n in out_pieces:
+            relay(0, n)
+
+    for j in range(2, ny - 1):
+        for n in in_pieces:
+            relay(j, n)
+
     @pl.when(between)
     def _():
         for i in range(2):
-
-            @pl.when(comes[i])
-            def _():
-                for g in range(2):
-                    hop1(i, g).wait_recv()
-                for c in spread1(i):
-                    c.start()
-                for g in range(2):
-                    first_in[i][g, mine, :] = HOP1[i, g]
-
-        prepare(0, b1[0], S1[0])
-
-    for j in range(1, ny - 1):
-        for n in in_pieces:
-            relay(j, n)
-
-    @pl.when(between)
-    def _():
-        for i in range(2):
-
-            @pl.when(comes[i])
-            def _():
-                for c in spread1_in(i):
-                    c.wait_recv()
-
-            @pl.when(edge[i])
-            def _():
-                own_in[i].wait()
-                guest_in[i].wait_recv()
+            for c in spread1_in(i):
+                c.wait_recv()
 
         guest_stash.wait_recv()
         guest_frames.wait_recv()
@@ -450,6 +461,23 @@
             squares = squares + jnp.sum(x.astype(F32) * x.astype(F32), -1, keepdims=True)
         MX[0:rows, :] = (mixed * lax.rsqrt(squares / width + 1e-05)).astype(BF)
         attend(0, allowed(fr[1:2]))
+
+    def block(i):
+        return jnp.where(y < ny // 2, i, ny - 1 - i)
+
+    def second_output(i):
+        b = block(i)
+        PP2[0, :, cols(b)] = nt(CT[0:rows, :], WO[cols(b), :]).astype(BF)
+        for c in send2(0, b):
+            c.start()
+
+    def second_grad(i):
+        b = block(i)
+        if i == 0:
+            pl.when(edge[1])(lambda: own_in2[1].wait())
+        pl.when(comes[1])(lambda: gathered2(1, b))
+        part = nn(G2[:, cols(b)], WO[cols(b), :])
+        DA[0:rows, :] = part if i == 0 else DA[0:rows, :] + part
 
     @pl.when(end)
     def _():
@@ -464,21 +492,30 @@
                 relay(j, n)
             for n in out_pieces:
                 from_sibling(j, n)
-        arrive(0)
-        second_forward()
+
+        @pl.when(jnp.logical_not(wrap))
+        def _():
+            arrive(0)
+            second_forward()
+            for i in range(ny - 1):
+                second_output(i)
+            arrive(1)
+
         for n in out_pieces:
             relay(ny - 2, n)
-        arrive(1)
+        pl.when(wrap)(lambda: arrive(1))
+        for i in range(ny - 1):
+            second_grad(i)
         for n in out_pieces:
             from_sibling(ny - 2, n)
+        pl.when(jnp.logical_not(wrap))(lambda: second_output(ny - 1))
+        second_grad(ny - 1)
 
     @pl.when(between)
     def _():
         project(0, b2 + rows)
         guest = FG[...].astype(F32)
         marks = (fr, guest)
-        for n in out_pieces:
-            relay(0, n)
         for g in range(2):
             attend(fw[g], allowed(marks[g][0:1]))
         for g in range(2):
@@ -520,33 +557,54 @@
             reduced1(0, b)
         for b in range(ny):
             reduced1(1, b)
-        arrive(0)
+        pl.when(jnp.logical_not(wrap))(lambda: arrive(0))
         keep_second()
         arrive(1)
-        second_forward()
-
-    for b in range(ny):
-        PP2[0, :, cols(b)] = nt(CT[0:rows, :], WO[cols(b), :]).astype(BF)
-        for c in send2(0, b):
-            c.start()
-    pl.when(edge[1])(lambda: own_in2[1].wait())
-    dctx = jnp.zeros((rows, qh * HS), F32)
-    for b in range(ny):
-        pl.when(comes[1])(lambda: gathered2(1, b))
-        dctx = dctx + nn(G2[:, cols(b)], WO[cols(b), :])
-    mean = heads_back(2, b2, 0, dctx.astype(BF))
-    for b in range(ny):
+
+        @pl.when(jnp.logical_not(wrap))
+        def _():
+            second_forward()
+            for i in range(ny):
+                second_output(i)
+
+        for i in range(ny):
+            second_grad(i)
+
+    def second_heads():
+        return heads_back(2, b2, 0, DA[0:rows, :].astype(BF))
+
+    def second_input(mean, b):
         PP2[1, :, cols(b)] = norm_back(2, nn(DM[0:rows, :], WT[:, cols(b)]), S2[:, cols(b)], mean)
         for c in send2(1, b):
             c.start()
-        if b % 2:
-            reduced2(0, b - 1)
-            reduced2(0, b)
+
+    @pl.when(jnp.logical_not(wrap))
+    def _():
+        mean = second_heads()
+        for b in range(ny):
+            second_input(mean, b)
+            if b % 2:
+                reduced2(0, b - 1)
+                reduced2(0, b)
+        for b in range(ny):
+            reduced2(1, b)
+
+    @pl.when(wrap)
+    def _():
+        arrive(0)
+        mean = second_heads()
+        for b in range(ny):
+            second_input(mean, b)
+        second_forward()
+        for i in range(ny):
+            second_output(i)
+        for i in (1, 0):
+            for b in range(ny):
+                reduced2(i, b)
+
     keep_f = pltpu.make_async_copy(SL2.at[0], out_f.at[0, mine], loc_sem.at[7])
+    keep_b = pltpu.make_async_copy(SL2.at[1], out_b.at[0, mine], loc_sem.at[8])
     keep_f.start()
-    for b in range(ny):
-        reduced2(1, b)
-    keep_b = pltpu.make_async_copy(SL2.at[1], out_b.at[0, mine], loc_sem.at[8])
     keep_b.start()
 
     for n in range(2 * PARTS):
@@ -565,10 +623,8 @@
 
         @pl.when(between)
         def _():
-            @pl.when(comes[i])
-            def _():
-                for c in spread1(i):
-                    c.wait_send()
+            for c in spread1(i):
+                c.wait_send()
 
             for b in range(ny):
                 for c in send1(i, b):
@@ -643,7 +699,7 @@
             dma((2, ny, 2 * PARTS)),
             dma((9,)),
             dma((4,)),
-            dma((4,)),
+            dma((2,)),
             dma((2,)),
             dma((2, 2)),
             dma((2, 2, ny)),
@@ -652,6 +708,7 @@
             dma((6, nt_ - 1, ny)),
             dma((4, nt_ - 1, ny)),
             dma((4, nt_ - 1, ny)),
+            pltpu.SemaphoreType.REGULAR,
         ],
         compiler_params=pltpu.CompilerParams(
             collective_id=0, has_side_effects=True, vmem_limit_bytes=60 << 20

time: 112 us -> 107 us (0.955)
  the two profiles are of different devices: /device:TPU:56 before, /device:TPU:216 now
where the time goes in v4:
time: 107 us
  Pallas kernels  104 us (97%)
  local copies, waits for them, and re-layouts  2.49 us (2%)
    pallas_call x1, Pallas kernels, body(): pl.pallas_call(kernel, out_shape=[jax.ShapeDtypeStruct(sent.shape, BF)] *...  104 us
    unnamed x4, local copies, waits for them, and re-layouts  2.49 us

profile of v4, /device:TPU:216, one launch (start us, length us, event | category | flops | bytes accessed | tf_op | source)
XLA Modules:
  0.0 107.3 jit_solution(10138144881747337404)
XLA Ops:
  0.6 104.2 %relay.1 = (bf16[1,64,2560]{2,1,0:T(8,128)(2,1)}, bf16[1,64,2560]{2,1,0:T(8,128)(2,1)}) custom-call(bf16[2,64,2560]{2,1,0:T(8,128)(2,1)} %fresh.1, bf16[1,64,2560]{2,1,0:T(8,128)(2,1)} %sent.1, bf16[1,2,64,2560]{3,2,1,0:T(8,128)(2,1)} %stash.1, bf16[1,64,2560]{2,1,0:T(8,128)(2,1)} %returned.1, bf16[2,64,2560]{2,1,0:T(8,128)(2,1)} %loss.1, s32[1,2]{1,0:T(1,128)} %plan.1, ...), custom_call_target="tpu_custom_call" | custom-call | tf_op jit(solution)/shard_map/relay/pallas_call | solution.py:669
  104.8 0.0 copy-start
  104.8 1.8 %copy.13 = bf16[1,64,2560]{2,1,0:T(8,128)(2,1)} copy(bf16[1,64,2560]{2,1,0:T(8,128)(2,1)} %get-tuple-element.4) | data formatting | bytes 655360
  106.6 0.0 copy-done
  106.6 0.7 copy.14
Async XLA Ops:
  104.8 1.8 %copy-start = (bf16[1,64,2560]{2,1,0:T(8,128)(2,1)S(1)}, bf16[1,64,2560]{2,1,0:T(8,128)(2,1)}, u32[]{:S(2)}) copy-start(bf16[1,64,2560]{2,1,0:T(8,128)(2,1)} %get-tuple-element.5) | copy-start | bytes 983044

commit v5 on v4

--- a/solution.py
+++ b/solution.py
@@ -492,24 +492,22 @@
                 relay(j, n)
             for n in out_pieces:
                 from_sibling(j, n)
+        for n in out_pieces[:-1]:
+            relay(ny - 2, n)
+        pl.when(jnp.logical_not(wrap))(lambda: arrive(0))
+        relay(ny - 2, out_pieces[-1])
+        arrive(1)
+        pl.when(jnp.logical_not(wrap))(second_forward)
+        for n in out_pieces:
+            from_sibling(ny - 2, n)
 
         @pl.when(jnp.logical_not(wrap))
         def _():
-            arrive(0)
-            second_forward()
-            for i in range(ny - 1):
+            for i in range(ny):
                 second_output(i)
-            arrive(1)
-
-        for n in out_pieces:
-            relay(ny - 2, n)
-        pl.when(wrap)(lambda: arrive(1))
-        for i in range(ny - 1):
+
+        for i in range(ny):
             second_grad(i)
-        for n in out_pieces:
-            from_sibling(ny - 2, n)
-        pl.when(jnp.logical_not(wrap))(lambda: second_output(ny - 1))
-        second_grad(ny - 1)
 
     @pl.when(between)
     def _():

time: 107 us -> 104 us (0.972)
  the two profiles are of different devices: /device:TPU:216 before, /device:TPU:56 now
where the time goes in v5:
time: 104 us
  Pallas kernels  100 us (96%)
  local copies, waits for them, and re-layouts  2.49 us (2%)
    pallas_call x1, Pallas kernels, body(): pl.pallas_call(kernel, out_shape=[jax.ShapeDtypeStruct(sent.shape, BF)] *...  100 us
    unnamed x4, local copies, waits for them, and re-layouts  2.49 us

profile of v5, /device:TPU:56, one launch (start us, length us, event | category | flops | bytes accessed | tf_op | source)
XLA Modules:
  0.0 103.5 jit_solution(5678111414136180581)
XLA Ops:
  0.6 100.4 %relay.1 = (bf16[1,64,2560]{2,1,0:T(8,128)(2,1)}, bf16[1,64,2560]{2,1,0:T(8,128)(2,1)}) custom-call(bf16[2,64,2560]{2,1,0:T(8,128)(2,1)} %fresh.1, bf16[1,64,2560]{2,1,0:T(8,128)(2,1)} %sent.1, bf16[1,2,64,2560]{3,2,1,0:T(8,128)(2,1)} %stash.1, bf16[1,64,2560]{2,1,0:T(8,128)(2,1)} %returned.1, bf16[2,64,2560]{2,1,0:T(8,128)(2,1)} %loss.1, s32[1,2]{1,0:T(1,128)} %plan.1, ...), custom_call_target="tpu_custom_call" | custom-call | tf_op jit(solution)/shard_map/relay/pallas_call | solution.py:667
  101.0 0.0 copy-start
  101.0 1.8 %copy.13 = bf16[1,64,2560]{2,1,0:T(8,128)(2,1)} copy(bf16[1,64,2560]{2,1,0:T(8,128)(2,1)} %get-tuple-element.4) | data formatting | bytes 655360
  102.8 0.0 copy-done
  102.8 0.7 copy.14
Async XLA Ops:
  101.0 1.8 %copy-start = (bf16[1,64,2560]{2,1,0:T(8,128)(2,1)S(1)}, bf16[1,64,2560]{2,1,0:T(8,128)(2,1)}, u32[]{:S(2)}) copy-start(bf16[1,64,2560]{2,1,0:T(8,128)(2,1)} %get-tuple-element.5) | copy-start | bytes 983044

commit v6 on v5

--- a/solution.py
+++ b/solution.py
@@ -135,7 +135,12 @@
         sib = remote(other, other, sib_send.at[d, j, n], sib_recv.at[d, j, n], fsdp=sibling)
         return valid, goes_on, got, nxt, over, sib
 
-    def relay(j, n):
+    def pass_on(j, n):
+        for d in range(2):
+            _, goes_on, _, nxt, _, _ = line(d, j, n)
+            pl.when(goes_on)(lambda: nxt.start())
+
+    def relay(j, n, hold=False):
         for d in range(2):
             valid, goes_on, got, nxt, over, _ = line(d, j, n)
 
@@ -143,7 +148,7 @@
             def _():
                 got.wait_recv()
 
-            if nxt is not None:
+            if nxt is not None and not hold:
                 pl.when(goes_on)(lambda: nxt.start())
             pl.when(valid)(lambda: over.start())
 
@@ -492,10 +497,9 @@
                 relay(j, n)
             for n in out_pieces:
                 from_sibling(j, n)
-        for n in out_pieces[:-1]:
+        pl.when(jnp.logical_not(wrap))(lambda: arrive(0))
+        for n in out_pieces:
             relay(ny - 2, n)
-        pl.when(jnp.logical_not(wrap))(lambda: arrive(0))
-        relay(ny - 2, out_pieces[-1])
         arrive(1)
         pl.when(jnp.logical_not(wrap))(second_forward)
         for n in out_pieces:
@@ -531,7 +535,7 @@
             elif i == 3:
                 for j in range(1, ny - 1):
                     for n in out_pieces:
-                        relay(j, n)
+                        relay(j, n, hold=n == out_pieces[-1])
                     for n in out_pieces:
                         from_sibling(j, n)
             b = jnp.where(y < ny // 2, order[i], ny - 1 - order[i])
@@ -553,6 +557,8 @@
                 c.start()
         for b in range(ny):
             reduced1(0, b)
+        for j in range(1, ny - 2):
+            pass_on(j, out_pieces[-1])
         for b in range(ny):
             reduced1(1, b)
         pl.when(jnp.logical_not(wrap))(lambda: arrive(0))
@@ -581,11 +587,9 @@
         mean = second_heads()
         for b in range(ny):
             second_input(mean, b)
-            if b % 2:
-                reduced2(0, b - 1)
-                reduced2(0, b)
-        for b in range(ny):
-            reduced2(1, b)
+        for i in range(2):
+            for j in range(ny):
+                reduced2(i, block(j) if i == 0 else j)
 
     @pl.when(wrap)
     def _():

time: 104 us -> 104 us (level)
  no operation moved by 1% of the time
where the time goes in v6:
time: 104 us
  Pallas kernels  100 us (96%)
  local copies, waits for them, and re-layouts  2.49 us (2%)
    pallas_call x1, Pallas kernels, body(): pl.pallas_call(kernel, out_shape=[jax.ShapeDtypeStruct(sent.shape, BF)] *...  100 us
    unnamed x4, local copies, waits for them, and re-layouts  2.49 us

profile of v6, /device:TPU:56, one launch (start us, length us, event | category | flops | bytes accessed | tf_op | source)
XLA Modules:
  0.0 103.5 jit_solution(583262001699794551)
XLA Ops:
  0.6 100.4 %relay.1 = (bf16[1,64,2560]{2,1,0:T(8,128)(2,1)}, bf16[1,64,2560]{2,1,0:T(8,128)(2,1)}) custom-call(bf16[2,64,2560]{2,1,0:T(8,128)(2,1)} %fresh.1, bf16[1,64,2560]{2,1,0:T(8,128)(2,1)} %sent.1, bf16[1,2,64,2560]{3,2,1,0:T(8,128)(2,1)} %stash.1, bf16[1,64,2560]{2,1,0:T(8,128)(2,1)} %returned.1, bf16[2,64,2560]{2,1,0:T(8,128)(2,1)} %loss.1, s32[1,2]{1,0:T(1,128)} %plan.1, ...), custom_call_target="tpu_custom_call" | custom-call | tf_op jit(solution)/shard_map/relay/pallas_call | solution.py:671
  101.0 0.0 copy-start
  101.0 1.8 %copy.13 = bf16[1,64,2560]{2,1,0:T(8,128)(2,1)} copy(bf16[1,64,2560]{2,1,0:T(8,128)(2,1)} %get-tuple-element.4) | data formatting | bytes 655360
  102.8 0.0 copy-done
  102.8 0.7 copy.14
Async XLA Ops:
  101.0 1.8 %copy-start = (bf16[1,64,2560]{2,1,0:T(8,128)(2,1)S(1)}, bf16[1,64,2560]{2,1,0:T(8,128)(2,1)}, u32[]{:S(2)}) copy-start(bf16[1,64,2560]{2,1,0:T(8,128)(2,1)} %get-tuple-element.5) | copy-start | bytes 983044

commit v7 on v6

--- a/solution.py
+++ b/solution.py
@@ -52,7 +52,6 @@
     between = jnp.logical_and(y > 0, y < ny - 1)
     end = jnp.logical_not(between)
     partner = jnp.where(jnp.logical_xor(y < ny // 2, between), f + 2, f - 2)
-    wrap = s == ns // 2
     above, below = jnp.minimum(s + 1, ns - 1), jnp.maximum(s - 1, 0)
 
     def cols(b):
@@ -497,18 +496,16 @@
                 relay(j, n)
             for n in out_pieces:
                 from_sibling(j, n)
-        pl.when(jnp.logical_not(wrap))(lambda: arrive(0))
+        arrive(0)
         for n in out_pieces:
             relay(ny - 2, n)
         arrive(1)
-        pl.when(jnp.logical_not(wrap))(second_forward)
+        second_forward()
         for n in out_pieces:
             from_sibling(ny - 2, n)
 
-        @pl.when(jnp.logical_not(wrap))
-        def _():
-            for i in range(ny):
-                second_output(i)
+        for i in range(ny):
+            second_output(i)
 
         for i in range(ny):
             second_grad(i)
@@ -549,27 +546,28 @@
             part = nn(grad, weight)
             DA[...] = part if i == 0 else DA[...] + part
         mean = [heads_back(g, b1[g], g * rows, DA[g * rows : (g + 1) * rows, :].astype(BF)) for g in range(2)]
+        blocks = [jnp.where(y < ny // 2, o, ny - 1 - o) for o in order]
+        last_block = blocks[3]
+        for i in range(3):
+            reduced1(0, blocks[i])
         for b in range(ny):
             dn = nn(DM[...], WT[:, cols(b)])
             for g in range(2):
                 PP1[1, g, :, cols(b)] = norm_back(g, dn[g * rows : (g + 1) * rows], S1[g, :, cols(b)], mean[g])
             for c in send1(1, b):
                 c.start()
-        for b in range(ny):
-            reduced1(0, b)
+        reduced1(0, last_block)
         for j in range(1, ny - 2):
             pass_on(j, out_pieces[-1])
         for b in range(ny):
             reduced1(1, b)
-        pl.when(jnp.logical_not(wrap))(lambda: arrive(0))
+        arrive(0)
         keep_second()
         arrive(1)
 
-        @pl.when(jnp.logical_not(wrap))
-        def _():
-            second_forward()
-            for i in range(ny):
-                second_output(i)
+        second_forward()
+        for i in range(ny):
+            second_output(i)
 
         for i in range(ny):
             second_grad(i)
@@ -582,27 +580,12 @@
         for c in send2(1, b):
             c.start()
 
-    @pl.when(jnp.logical_not(wrap))
-    def _():
-        mean = second_heads()
-        for b in range(ny):
-            second_input(mean, b)
-        for i in range(2):
-            for j in range(ny):
-                reduced2(i, block(j) if i == 0 else j)
-
-    @pl.when(wrap)
-    def _():
-        arrive(0)
-        mean = second_heads()
-        for b in range(ny):
-            second_input(mean, b)
-        second_forward()
-        for i in range(ny):
-            second_output(i)
-        for i in (1, 0):
-            for b in range(ny):
-                reduced2(i, b)
+    mean = second_heads()
+    for b in range(ny):
+        second_input(mean, b)
+    for i in range(2):
+        for j in range(ny):
+            reduced2(i, block(j) if i == 0 else j)
 
     keep_f = pltpu.make_async_copy(SL2.at[0], out_f.at[0, mine], loc_sem.at[7])
     keep_b = pltpu.make_async_copy(SL2.at[1], out_b.at[0, mine], loc_sem.at[8])

time: 104 us -> 105 us (level)
  no operation moved by 1% of the time
where the time goes in v7:
time: 105 us; the launch traced here: 104 us
  Pallas kernels  101 us (96%)
  local copies, waits for them, and re-layouts  2.49 us (2%)
    pallas_call x1, Pallas kernels, body(): pl.pallas_call(kernel, out_shape=[jax.ShapeDtypeStruct(sent.shape, BF)] *...  101 us
    unnamed x4, local copies, waits for them, and re-layouts  2.49 us

profile of v7, /device:TPU:56, one launch (start us, length us, event | category | flops | bytes accessed | tf_op | source)
XLA Modules:
  0.0 103.7 jit_solution(11329456060589689611)
XLA Ops:
  0.6 100.5 %relay.1 = (bf16[1,64,2560]{2,1,0:T(8,128)(2,1)}, bf16[1,64,2560]{2,1,0:T(8,128)(2,1)}) custom-call(bf16[2,64,2560]{2,1,0:T(8,128)(2,1)} %fresh.1, bf16[1,64,2560]{2,1,0:T(8,128)(2,1)} %sent.1, bf16[1,2,64,2560]{3,2,1,0:T(8,128)(2,1)} %stash.1, bf16[1,64,2560]{2,1,0:T(8,128)(2,1)} %returned.1, bf16[2,64,2560]{2,1,0:T(8,128)(2,1)} %loss.1, s32[1,2]{1,0:T(1,128)} %plan.1, ...), custom_call_target="tpu_custom_call" | custom-call | tf_op jit(solution)/shard_map/relay/pallas_call | solution.py:654
  101.2 0.0 copy-start
  101.2 1.8 %copy.13 = bf16[1,64,2560]{2,1,0:T(8,128)(2,1)} copy(bf16[1,64,2560]{2,1,0:T(8,128)(2,1)} %get-tuple-element.4) | data formatting | bytes 655360
  103.0 0.0 copy-done
  103.0 0.7 copy.14
Async XLA Ops:
  101.2 1.8 %copy-start = (bf16[1,64,2560]{2,1,0:T(8,128)(2,1)S(1)}, bf16[1,64,2560]{2,1,0:T(8,128)(2,1)}, u32[]{:S(2)}) copy-start(bf16[1,64,2560]{2,1,0:T(8,128)(2,1)} %get-tuple-element.5) | copy-start | bytes 983044
